TPU v7x, 512 devices: a whole 4x4x16 slice. The times are simulated.
512 devices in a mesh: dp: 16 (over z), expert: 32 (over x, y, core).
Axes of the slice: x: 4, y: 4, z: 16, core: 2. Of those that a mesh axis runs over, the one named last changes fastest.
Arguments:
- learn_hidden: bfloat16 [16, 128, 32, 1024], P('dp', 'expert'), may hold values from -6 to 6
- learn_cotangent: bfloat16 [16, 128, 32, 4096], P('dp', 'expert'), may hold values from -6 to 6
- master_blocks: float32 [32, 16, 2, 128, 128], P('expert', 'dp'), may hold values from -0.1875 to 0.1875
- changed: int32 [32, 16, 2], replicated, may hold values from 0 to 63, as said below
- rollout_slot: int32 [128], replicated, may hold values from 0 to 127, as said below
- rollout_weight: bfloat16 [128, 1024, 4096], P('expert', None, 'dp'), may hold values from -448 to 448
- rollout_scale: bfloat16 [128, 8, 32], P('expert', None, 'dp'), may hold values from 0.00014972687 to 0.00059890747
- decode_hidden: bfloat16 [2, 2048, 1024], P(None, 'expert'), may hold values from -6 to 6
- decode_routes: int32 [2, 2048, 8], P(None, 'expert'), may hold values from 0 to 127, all different within a row; in each aligned block of 64 rows (0 to 63, 64 to 127, ..., all dimensions but the last counted through in order) at most 8 rows name the same one
- decode_gates: float32 [2, 2048, 8], P(None, 'expert'), may hold values from 0.05 to 0.5
Outputs:
- decode_out: bfloat16 [2, 2048, 4096], P(None, 'expert', 'dp')
Inputs may be any that keep to these rules, and one draw needn't show every extreme that they name: `changed`: for each learner index j and group g the 2 codes differ; code k names expert j * 4 + k // 16, block row (k // 2) % 8 and block column g * 2 + k % 2. `rollout_slot`: each expert has its own row. `decode_routes`: each token names 8 different experts. Among the 64 tokens of one index of expert in one step no expert is named by more than 8 tokens, a bound that some block reaches.
All inputs are finite; a program needn't handle non-finite values.
Results may differ from a plain program's by a relative error of at most 0.006.
Values may be sent and summed in bfloat16 or wider, within the bound.
No kernel may reach another device: no remote copies, remote signals or barrier semaphores. Data moves between devices by JAX's collectives and lax.ppermute only.
A program may use at most 64 MiB of HBM per device.

v0:
```python
import math

import jax
import jax.numpy as jnp
from jax import lax
from jax.sharding import PartitionSpec as P

learning_rate = 0.03
quant_limit = 448.0
epsilon_value = 1e-06


def quantize(updated):
    peak = jnp.max(jnp.abs(updated), axis=(-2, -1))
    block_scale = ((peak + epsilon_value) / quant_limit).astype(jnp.bfloat16)
    packed = (updated / block_scale.astype(jnp.float32)[..., None, None]).astype(jnp.bfloat16)
    return (packed, block_scale)


def shards(
    learn_hidden,
    learn_cotangent,
    master_blocks,
    changed,
    rollout_slot,
    rollout_weight,
    rollout_scale,
    decode_hidden,
    decode_routes,
    decode_gates,
):
    dp_count = lax.axis_size("dp")
    expert_count = lax.axis_size("expert")
    dp_index = lax.axis_index("dp")
    expert_index = lax.axis_index("expert")
    exp_dev = learn_hidden.shape[1]
    learn_rows = learn_hidden.shape[2]
    width_ff = learn_hidden.shape[3]
    width_d = learn_cotangent.shape[3]
    block_size = master_blocks.shape[-1]
    per_group = master_blocks.shape[2]
    row_blocks = width_ff // block_size
    col_blocks = width_d // block_size
    col_local = col_blocks // dp_count
    hidden_tiles = (
        learn_hidden[0]
        .reshape(exp_dev, learn_rows, row_blocks, block_size)
        .transpose(0, 2, 1, 3)
        .reshape(exp_dev * row_blocks, learn_rows, block_size)
    )
    cotangent_tiles = (
        learn_cotangent[0]
        .reshape(exp_dev, learn_rows, col_blocks, block_size)
        .transpose(0, 2, 1, 3)
        .reshape(exp_dev * col_blocks, learn_rows, block_size)
    )
    own_codes = lax.dynamic_index_in_dim(changed, expert_index, 0, keepdims=False).reshape(-1)
    column_group = jnp.arange(per_group * lax.axis_size("dp"), dtype=jnp.int32) // per_group
    local_expert = own_codes // (row_blocks * col_local)
    block_row = own_codes // col_local % row_blocks
    block_col = column_group * col_local + own_codes % col_local
    hidden_tile = jnp.take(hidden_tiles, local_expert * row_blocks + block_row, axis=0)
    cotangent_tile = jnp.take(cotangent_tiles, local_expert * col_blocks + block_col, axis=0)
    gradient = lax.psum_scatter(
        jnp.einsum("nrp,nrq->npq", hidden_tile, cotangent_tile, preferred_element_type=jnp.float32),
        "dp",
        scatter_dimension=0,
        tiled=True,
    )
    updated = master_blocks[0, 0] - learning_rate / math.sqrt(dp_count * learn_rows) * gradient
    pieces = lax.all_gather(updated[None], "expert", axis=0, tiled=True)
    block_count = pieces.shape[0] * per_group
    packed_blocks, scale_values = quantize(pieces.reshape(block_count, block_size, block_size))
    weights = rollout_weight
    scales = rollout_scale
    block_count = packed_blocks.shape[0]
    block_index = jnp.arange(block_count, dtype=jnp.int32)
    source = block_index // per_group
    slot_within = block_index % per_group
    block_code = changed[source, dp_index, slot_within]
    local_expert = block_code // (row_blocks * col_local)
    block_row = block_code // col_local % row_blocks
    block_col = block_code % col_local
    where_at = rollout_slot[source * exp_dev + local_expert]
    is_owned = where_at // exp_dev == expert_index
    target = jnp.where(is_owned, where_at % exp_dev, exp_dev)
    width_now = weights.shape[2]
    tiled = weights.reshape(exp_dev, row_blocks, block_size, width_now // block_size, block_size)
    tiled = tiled.at[target, block_row, :, block_col, :].set(packed_blocks, mode="drop")
    scales = scales.at[target, block_row, block_col].set(scale_values, mode="drop")
    refreshed = (tiled.reshape(weights.shape), scales)
    weights, scales = refreshed
    width_local = weights.shape[2]
    weight_tiles = weights.reshape(exp_dev, row_blocks, block_size, width_local)
    scale_cols = jnp.repeat(scales.astype(jnp.float32), block_size, axis=2)
    tok_dev = decode_hidden.shape[1]
    top_count = decode_routes.shape[2]
    experts_all = rollout_slot.shape[0]
    capacity = min(tok_dev, max(2, 2 * tok_dev * top_count // experts_all))
    slot_count = expert_count * exp_dev * capacity
    expert_ids = jnp.arange(experts_all, dtype=jnp.int32)
    outputs = []
    for section_index in range(2):
        flattened = decode_routes[section_index].reshape(-1)
        onehot = (flattened[:, None] == expert_ids[None, :]).astype(jnp.int32)
        position = jnp.sum(onehot * rollout_slot[None, :], axis=1)
        placed = (position[:, None] == expert_ids[None, :]).astype(jnp.int32)
        before = jnp.cumsum(placed, axis=0) - placed
        rank_within = jnp.sum(before * placed, axis=1)
        slot_index = position * capacity + rank_within
        selector = jnp.any(
            slot_index.reshape(tok_dev, top_count)[None, :, :]
            == jnp.arange(slot_count, dtype=jnp.int32)[:, None, None],
            axis=2,
        )
        outgoing = jnp.dot(
            selector.astype(jnp.bfloat16),
            decode_hidden[section_index],
            preferred_element_type=jnp.float32,
        ).astype(jnp.bfloat16)
        outgoing = outgoing.reshape(expert_count, exp_dev, capacity, width_ff)
        arrived = lax.all_to_all(outgoing, "expert", split_axis=0, concat_axis=2, tiled=True)
        expert_arrived = arrived[0]
        row_total = expert_arrived.shape[1]
        partial_value = jnp.einsum(
            "erbf,ebfc->erbc",
            expert_arrived.reshape(exp_dev, row_total, row_blocks, block_size),
            weight_tiles,
            preferred_element_type=jnp.float32,
        )
        expert_rows = jnp.sum(partial_value * scale_cols[:, None, :, :], axis=2).astype(
            jnp.bfloat16
        )
        returned = lax.all_to_all(
            expert_rows[None], "expert", split_axis=2, concat_axis=0, tiled=True
        )
        picked = jnp.take(returned.reshape(slot_count, width_local), slot_index, axis=0)
        weighted = (
            picked.reshape(tok_dev, top_count, width_local).astype(jnp.float32)
            * decode_gates[section_index][:, :, None]
        )
        outputs.append(jnp.sum(weighted, axis=1).astype(jnp.bfloat16))
    return jnp.stack(outputs)


def solution(mesh):
    return jax.shard_map(
        shards,
        mesh=mesh,
        in_specs=(
            P("dp", "expert", None, None),
            P("dp", "expert", None, None),
            P("expert", "dp", None, None, None),
            P(),
            P(),
            P("expert", None, "dp"),
            P("expert", None, "dp"),
            P(None, "expert", None),
            P(None, "expert", None),
            P(None, "expert", None),
        ),
        out_specs=P(None, "expert", "dp"),
        check_vma=False,
    )
```

profile of v0, /device:TPU:1, one launch (start us, length us, event | category | flops | bytes accessed | tf_op | source)
XLA Modules:
  0.0 250.1 jit_solution(10055509584467739032)
XLA Ops:
  11.7 1.9 fusion.14
  13.7 68.0 %reduce-scatter.2.cloned.1.call-done = f32[2,128,128]{2,1,0:T(8,128)} async-done(((f32[32,128,128]{2,1,0:T(8,128)}), f32[2,128,128]{2,1,0:T(8,128)}) %reduce-scatter.2.cloned.1.call-update) | async-done | bytes 131088 | tf_op jit(solution)/shard_map/reduce_scatter | solution.py:64
  86.1 2.1 convolution_convert_fusion.1
  88.2 18.2 %all-to-all-start = ((bf16[32,4,8,1024]{3,2,1,0:T(8,128)(2,1)}), bf16[32,4,8,1024]{3,2,1,0:T(8,128)(2,1)S(1)}, u32[]{:S(2)}, u32[]{:S(2)}) async-start(bf16[32,4,8,1024]{3,2,1,0:T(8,128)(2,1)} %bitcast.167), calls=%async_computation.1 | async-start | bytes 4194304 | tf_op jit(solution)/shard_map/all_to_all | solution.py:122
  108.2 2.1 convolution_convert_fusion
  110.3 26.3 %all-to-all-done = bf16[32,4,8,1024]{3,2,1,0:T(8,128)(2,1)S(1)} async-done(((bf16[32,4,8,1024]{3,2,1,0:T(8,128)(2,1)}), bf16[32,4,8,1024]{3,2,1,0:T(8,128)(2,1)S(1)}, u32[]{:S(2)}, u32[]{:S(2)}) %all-to-all-start) | async-done | bytes 2097184 | tf_op jit(solution)/shard_map/all_to_all | solution.py:122
  138.0 5.2 %all-to-all-start.2 = ((bf16[32,4,8,1024]{3,2,1,0:T(8,128)(2,1)}), bf16[32,4,8,1024]{3,2,1,0:T(8,128)(2,1)}, u32[]{:S(2)}, u32[]{:S(2)}) async-start(bf16[32,4,8,1024]{3,2,1,0:T(8,128)(2,1)} %bitcast.166), calls=%async_computation.3 | async-start | bytes 4194304 | tf_op jit(solution)/shard_map/all_to_all | solution.py:122
  144.0 4.0 %reshape.822 = bf16[4,8,128,2,128]{4,3,2,1,0:T(2,128)(2,1)} reshape(bf16[4,1024,256]{2,1,0:T(8,128)(2,1)} %param.17) | data formatting | bytes 4194304 | tf_op jit(solution)/shard_map/reshape | solution.py:88
  148.0 2.6 %copy.86 = bf16[4,8,128,2,128]{4,2,3,1,0:T(8,128)(2,1)S(1)} copy(bf16[4,8,128,2,128]{4,3,2,1,0:T(2,128)(2,1)} %reshape.822) | data formatting | bytes 4194304 | tf_op jit(solution)/shard_map/reshape | solution.py:88
  150.9 2.0 copy.109
  152.9 27.3 %all-gather.3.cloned.1.call-done = f32[64,128,128]{2,1,0:T(8,128)} async-done(((f32[2,128,128]{2,1,0:T(8,128)}), f32[64,128,128]{2,1,0:T(8,128)}) %all-gather.3.cloned.1.call-update) | async-done | bytes 4194320 | tf_op jit(solution)/shard_map/all_gather | solution.py:71
  180.2 2.9 %abs_reduce_fusion = f32[64]{0:T(128)S(1)} fusion(f32[64,128,128]{2,1,0:T(8,128)} %all-gather.3.cloned.1.call-done), kind=kLoop, calls=%fused_computation.10 | loop fusion | flops 2097088 | bytes 4194560 | tf_op jit(solution)/shard_map/reduce_max | solution.py:14
  183.7 2.0 divide_convert_fusion
  185.6 8.0 %scatter_fusion = bf16[4,8,128,2,128]{4,2,3,1,0:T(8,128)(2,1)S(1)} fusion(bf16[4,8,128,2,128]{4,2,3,1,0:T(8,128)(2,1)S(1)} %copy.86, s32[64]{0:T(128)S(1)} %fusion.49, bf16[64,128,128]{2,1,0:T(8,128)(2,1)} %divide_convert_fusion), kind=kCustom, calls=%fused_computation.6 | custom fusion | bytes 6292224 | tf_op jit(solution)/shard_map/scatter | solution.py:89
  193.6 2.6 %copy.87 = bf16[4,8,128,2,128]{2,4,3,1,0:T(8,128)(2,1)} copy(bf16[4,8,128,2,128]{4,2,3,1,0:T(8,128)(2,1)S(1)} %scatter_fusion) | data formatting | bytes 4194304 | tf_op jit(solution)/shard_map/scatter | solution.py:89
  196.3 4.4 %scatter_fusion.1 = bf16[4,8,2]{1,0,2:T(4,128)(2,1)S(1)} fusion(bf16[4,8,2]{1,0,2:T(4,128)(2,1)S(1)} %copy.90, s32[64]{0:T(128)S(1)} %fusion.49, bf16[64]{0:T(256)(128)(2,1)S(1)} %get-tuple-element.21), kind=kCustom, calls=%fused_computation.7 | custom fusion | bytes 1152 | tf_op jit(solution)/shard_map/scatter | solution.py:90
  200.8 3.5 %multiply_reduce_fusion.1 = bf16[4,256,256]{2,1,0:T(8,128)(2,1)S(1)} fusion(f32[4,8,256]{2,1,0:T(8,128)S(1)} %broadcast_bitcast_fusion, bf16[4,8,128,256]{2,3,1,0:T(8,128)(2,1)} %bitcast.171, bf16[4,256,8,128]{3,2,1,0:T(8,128)(2,1)} %bitcast.173), kind=kOutput, calls=%fused_computation.9 | convolution fusion | flops 540803072 | bytes 4751360 | tf_op jit(solution)/shard_map/erbf,ebfc->erbc/dot_general | solution.py:125
  205.4 5.8 %all-to-all-start.1 = ((bf16[1,4,256,256]{3,1,0,2:T(4,128)(2,1)}), bf16[1,4,256,256]{3,1,0,2:T(4,128)(2,1)S(1)}, u32[]{:S(2)}, u32[]{:S(2)}) async-start(bf16[1,4,256,256]{3,1,0,2:T(4,128)(2,1)} %copy.92), calls=%async_computation.2 | async-start | bytes 1048576 | tf_op jit(solution)/shard_map/all_to_all | solution.py:134
  211.2 1.8 copy.99
  217.2 5.6 %all-to-all-done.1 = bf16[1,4,256,256]{3,1,0,2:T(4,128)(2,1)S(1)} async-done(((bf16[1,4,256,256]{3,1,0,2:T(4,128)(2,1)}), bf16[1,4,256,256]{3,1,0,2:T(4,128)(2,1)S(1)}, u32[]{:S(2)}, u32[]{:S(2)}) %all-to-all-start.1) | async-done | bytes 524320 | tf_op jit(solution)/shard_map/all_to_all | solution.py:134
  222.8 3.7 %all-to-all-start.3 = ((bf16[1,4,256,256]{3,1,0,2:T(4,128)(2,1)}), bf16[1,4,256,256]{3,1,0,2:T(4,128)(2,1)S(1)}, u32[]{:S(2)}, u32[]{:S(2)}) async-start(bf16[1,4,256,256]{3,1,0,2:T(4,128)(2,1)} %copy.101), calls=%async_computation.4 | async-start | bytes 1048576 | tf_op jit(solution)/shard_map/all_to_all | solution.py:134
  226.8 11.2 %all-to-all-done.3 = bf16[1,4,256,256]{3,1,0,2:T(4,128)(2,1)S(1)} async-done(((bf16[1,4,256,256]{3,1,0,2:T(4,128)(2,1)}), bf16[1,4,256,256]{3,1,0,2:T(4,128)(2,1)S(1)}, u32[]{:S(2)}, u32[]{:S(2)}) %all-to-all-start.3) | async-done | bytes 524320 | tf_op jit(solution)/shard_map/all_to_all | solution.py:134
  238.2 2.0 gather_fusion.4
  240.2 2.0 gather_fusion.5
  (105 shorter events, 21.1 us)
Async XLA Ops:
  6.5 0.7 copy-start
  6.5 75.2 %reduce-scatter.2.cloned.1.call-start = ((), (), s32[]{:S(2)}) async-start(), calls=%async_computation.5 | async-start | bytes 2228224 | tf_op jit(solution)/shard_map/reduce_scatter | solution.py:64
  9.4 1.0 copy-start.7
  11.7 70.0 %copy-start.8 = (f32[1,1,2,128,128]{4,3,2,1,0:T(8,128)S(1)}, f32[1,1,2,128,128]{4,3,2,1,0:T(8,128)}, u32[]{:S(2)}) copy-start(f32[1,1,2,128,128]{4,3,2,1,0:T(8,128)} %param.14) | copy-start | bytes 393220
  11.7 71.6 %copy-start.9 = (s32[2,64,8]{1,2,0:T(8,128)S(1)}, s32[2,64,8]{1,2,0:T(8,128)}, u32[]{:S(2)}) copy-start(s32[2,64,8]{1,2,0:T(8,128)} %param.20) | copy-start | bytes 12292
  11.7 72.0 %copy-start.1 = (s32[128]{0:T(128)S(1)}, s32[128]{0:T(128)}, u32[]{:S(2)}) copy-start(s32[128]{0:T(128)} %param.16) | copy-start | bytes 1540
  13.7 72.5 %copy-start.6 = (bf16[2,64,1024]{2,1,0:T(8,128)(2,1)S(1)}, bf16[2,64,1024]{2,1,0:T(8,128)(2,1)}, u32[]{:S(2)}) copy-start(bf16[2,64,1024]{2,1,0:T(8,128)(2,1)} %param.19) | copy-start | bytes 786436
  13.7 166.5 %all-gather.3.cloned.1.call-start = ((), (), s32[]{:S(2)}) async-start(), calls=%async_computation.6 | async-start | bytes 4325376 | tf_op jit(solution)/shard_map/all_gather | solution.py:71
  88.2 48.4 %all-to-all-start = ((bf16[32,4,8,1024]{3,2,1,0:T(8,128)(2,1)}), bf16[32,4,8,1024]{3,2,1,0:T(8,128)(2,1)S(1)}, u32[]{:S(2)}, u32[]{:S(2)}) async-start(bf16[32,4,8,1024]{3,2,1,0:T(8,128)(2,1)} %bitcast.167), calls=%async_computation.1 | async-start | bytes 4194304 | tf_op jit(solution)/shard_map/all_to_all | solution.py:122
  136.6 1.4 copy-start.3
  138.0 67.4 %all-to-all-start.2 = ((bf16[32,4,8,1024]{3,2,1,0:T(8,128)(2,1)}), bf16[32,4,8,1024]{3,2,1,0:T(8,128)(2,1)}, u32[]{:S(2)}, u32[]{:S(2)}) async-start(bf16[32,4,8,1024]{3,2,1,0:T(8,128)(2,1)} %bitcast.166), calls=%async_computation.3 | async-start | bytes 4194304 | tf_op jit(solution)/shard_map/all_to_all | solution.py:122
  148.0 2.6 %copy-start.11 = (bf16[4,8,2]{1,2,0:T(2,128)(2,1)S(1)}, bf16[4,8,2]{1,2,0:T(2,128)(2,1)}, u32[]{:S(2)}) copy-start(bf16[4,8,2]{1,2,0:T(2,128)(2,1)} %param.18) | copy-start | bytes 388
  148.0 2.6 %copy-start.4 = (bf16[32,4,8,1024]{3,2,1,0:T(8,128)(2,1)S(1)}, bf16[32,4,8,1024]{3,2,1,0:T(8,128)(2,1)}, u32[]{:S(2)}) copy-start(bf16[32,4,8,1024]{3,2,1,0:T(8,128)(2,1)} %copy-done.3) | copy-start | bytes 6291460
  180.2 3.4 %copy-start.2 = (f32[64,128,128]{2,1,0:T(8,128)S(1)}, f32[64,128,128]{2,1,0:T(8,128)}, u32[]{:S(2)}) copy-start(f32[64,128,128]{2,1,0:T(8,128)} %all-gather.3.cloned.1.call-done) | copy-start | bytes 12582916
  204.3 6.9 %copy-start.10 = (f32[2,64,8]{1,2,0:T(8,128)S(1)}, f32[2,64,8]{1,2,0:T(8,128)}, u32[]{:S(2)}) copy-start(f32[2,64,8]{1,2,0:T(8,128)} %param.21) | copy-start | bytes 12292
  205.4 17.4 %all-to-all-start.1 = ((bf16[1,4,256,256]{3,1,0,2:T(4,128)(2,1)}), bf16[1,4,256,256]{3,1,0,2:T(4,128)(2,1)S(1)}, u32[]{:S(2)}, u32[]{:S(2)}) async-start(bf16[1,4,256,256]{3,1,0,2:T(4,128)(2,1)} %copy.92), calls=%async_computation.2 | async-start | bytes 1048576 | tf_op jit(solution)/shard_map/all_to_all | solution.py:134
  213.0 1.6 copy-start.5
  222.8 15.3 %all-to-all-start.3 = ((bf16[1,4,256,256]{3,1,0,2:T(4,128)(2,1)}), bf16[1,4,256,256]{3,1,0,2:T(4,128)(2,1)S(1)}, u32[]{:S(2)}, u32[]{:S(2)}) async-start(bf16[1,4,256,256]{3,1,0,2:T(4,128)(2,1)} %copy.101), calls=%async_computation.4 | async-start | bytes 1048576 | tf_op jit(solution)/shard_map/all_to_all | solution.py:134
Sparse Core Ops, SparseCore 0:
  13.8 67.8 reduce-scatter.1
  84.8 95.3 all-gather.2
where the time goes:
time: 251 us; the launch traced here: 250 us
  waiting for transfers between devices  138 us (55%)
  local copies, waits for them, and re-layouts  43.2 us (17%)
  starting transfers between devices  32.9 us (13%)
  between operations  13.9 us (6%)
  matrix products  11.2 us (4%)
  other arithmetic  10.5 us (4%)
    reduce_scatter x1, waiting for transfers between devices, shards(): lax.psum_scatter(jnp.einsum('nrp,nrq->npq', hidden_tile, cotangent_tile,...  68 us
    all_gather x1, waiting for transfers between devices, shards(): pieces = lax.all_gather(updated[None], 'expert', axis=0, tiled=True)  27.3 us
    all_to_all x2, waiting for transfers between devices, shards(): lax.all_to_all(outgoing, 'expert', split_axis=0, concat_axis=2, tiled=True)  26.3 us
    all_to_all x2, starting transfers between devices, shards(): lax.all_to_all(outgoing, 'expert', split_axis=0, concat_axis=2, tiled=True)  23.4 us
    all_to_all x2, waiting for transfers between devices, shards(): lax.all_to_all(expert_rows[None], 'expert', split_axis=2, concat_axis=0,...  16.8 us
    scatter x2, local copies, waits for them, and re-layouts, shards(): tiled.at[target, block_row, :, block_col, :].set(packed_blocks, mode='drop')  10.6 us
    all_to_all x2, starting transfers between devices, shards(): lax.all_to_all(expert_rows[None], 'expert', split_axis=2, concat_axis=0,...  9.46 us
    unnamed x31, local copies, waits for them, and re-layouts  8.17 us
  transfers between devices with their start and end apart: 6, of which 5 were waited for; matrix products, arithmetic and copies ran while one was open for 19% of the time, Pallas kernels for 0%

commit v1 on v0

v1 whole, which is shorter than its diff:
```python
import functools
import math

import jax
import jax.numpy as jnp
from jax import lax
from jax.experimental import pallas as pl
from jax.experimental.pallas import tpu as pltpu
from jax.sharding import PartitionSpec as P

learning_rate = 0.03
quant_limit = 448.0
epsilon_value = 1e-06

SIDE = 4
CORES = 2
BLK = 128
SHIFTS = (1, 3, 2)
VMEM = pltpu.VMEM
SMEM = pltpu.SMEM


def vmem():
    return pl.BlockSpec(memory_space=VMEM)


def smem():
    return pl.BlockSpec(memory_space=SMEM)


def line_shift(stage, shift):
    pairs = []
    for x in range(SIDE):
        for y in range(SIDE):
            for core in range(CORES):
                if (core == 0) == (stage == 0):
                    to = (x, (y + shift) % SIDE)
                else:
                    to = ((x + shift) % SIDE, y)
                pairs.append(((x * SIDE + y) * CORES + core, (to[0] * SIDE + to[1]) * CORES + core))
    return pairs


def core_swap():
    return [(i, i ^ 1) for i in range(SIDE * SIDE * CORES)]


def same_core():
    return [[2 * i + core for i in range(SIDE * SIDE)] for core in range(CORES)]


def select_kernel(code_ref, hidden_ref, cotangent_ref, out_ref):
    groups, per_group = out_ref.shape[0], out_ref.shape[1]
    for g in range(groups):
        for c in range(per_group):
            k = code_ref[g * per_group + c]
            e = k >> 4
            r = (k >> 1) & 7
            b = (k & 1) + 2 * g
            out_ref[g, c, 0] = hidden_ref[e, :, pl.ds(pl.multiple_of(r * BLK, BLK), BLK)]
            out_ref[g, c, 1] = cotangent_ref[e, :, pl.ds(pl.multiple_of(b * BLK, BLK), BLK)]


def chunk_kernel(token_ref, route_ref, gate_ref, out_ref):
    tokens = token_ref.shape[0] * token_ref.shape[1]
    top = route_ref.shape[2]
    out_ref[0:tokens, :] = token_ref[...].reshape(tokens, token_ref.shape[2])
    route = route_ref[...].reshape(tokens, top).astype(jnp.float32)
    gate = gate_ref[...].reshape(tokens, top)
    high = gate.astype(jnp.bfloat16)
    low = (gate - high.astype(jnp.float32)).astype(jnp.bfloat16)
    same = lax.broadcasted_iota(jnp.int32, (tokens, tokens), 0) == lax.broadcasted_iota(
        jnp.int32, (tokens, tokens), 1
    )
    eye = same.astype(jnp.float32).astype(jnp.bfloat16)

    def turned(v):
        return lax.dot_general(
            v, eye, (((0,), (0,)), ((), ())), preferred_element_type=jnp.float32
        )

    out_ref[tokens : tokens + 16, 0:BLK] = jnp.concatenate(
        [turned(route.astype(jnp.bfloat16)), turned(high)], axis=0
    ).astype(jnp.bfloat16)
    out_ref[tokens : tokens + 16, BLK : 2 * BLK] = jnp.concatenate(
        [turned(low), jnp.zeros((8, BLK), jnp.float32)], axis=0
    ).astype(jnp.bfloat16)
    out_ref[tokens : tokens + 16, 2 * BLK :] = jnp.zeros(
        (16, out_ref.shape[1] - 2 * BLK), jnp.bfloat16
    )


def gate_columns(x_ref, q, ids):
    extra = x_ref[q, 128:144, 0 : 2 * BLK].astype(jnp.float32)
    route = extra[0:8, 0:BLK]
    gate = extra[8:16, 0:BLK] + extra[0:8, BLK : 2 * BLK]
    rows = [
        jnp.sum(jnp.where(route == e.astype(jnp.float32), gate, 0.0), axis=0, keepdims=True)
        for e in ids
    ]
    rows.append(jnp.zeros((16 - len(ids), BLK), jnp.float32))
    return jnp.transpose(jnp.concatenate(rows, axis=0))


def main_kernel(id_ref, x_ref, own_ref, other_ref, out_ref, picked_ref):
    chunks = x_ref.shape[0]
    rows = chunks * BLK
    ids = [id_ref[i] for i in range(12)]
    columns = jnp.concatenate([gate_columns(x_ref, q, ids) for q in range(chunks)], axis=0)
    x = x_ref[:, 0:BLK, :].reshape(rows, x_ref.shape[2])
    total = None
    for e in range(8):
        weight = own_ref[e] if e < 4 else other_ref[e - 4]
        part = jnp.dot(x, weight, preferred_element_type=jnp.float32) * columns[:, e : e + 1]
        total = part if total is None else total + part
    out_ref[...] = total
    for c in range(4):
        r = id_ref[12 + c]
        tile = x_ref[:, 0:BLK, pl.ds(pl.multiple_of(r * BLK, BLK), BLK)].reshape(rows, BLK)
        gated = tile.astype(jnp.float32) * columns[:, 8 + c : 9 + c]
        picked_ref[c] = gated.astype(jnp.bfloat16)


def refresh_kernel(recv_ref, master_ref, out_ref, *, step_size):
    groups, per_group = recv_ref.shape[0], recv_ref.shape[1]
    rows = groups * recv_ref.shape[3]
    for c in range(per_group):
        left = recv_ref[:, c, 0].reshape(rows, BLK)
        right = recv_ref[:, c, 1].reshape(rows, BLK)
        gradient = lax.dot_general(
            left, right, (((0,), (0,)), ((), ())), preferred_element_type=jnp.float32
        )
        updated = master_ref[c] - step_size * gradient
        peak = jnp.max(jnp.max(jnp.abs(updated), axis=0, keepdims=True), axis=1, keepdims=True)
        scale = ((peak + epsilon_value) / quant_limit).astype(jnp.bfloat16)
        scale = jnp.broadcast_to(scale.astype(jnp.float32), (16, BLK))
        out_ref[c, 0:BLK, :] = (updated / scale[0:1, :]).astype(jnp.bfloat16)
        out_ref[c, BLK : BLK + 16, :] = scale.astype(jnp.bfloat16)


def combine_kernel(
    place_ref, own_ref, other_ref, m0, m1, m2, m3, p0, p1, p2, p3, out_ref, total
):
    for i, (m_ref, p_ref) in enumerate(((m0, p0), (m1, p1), (m2, p2), (m3, p3))):
        total[...] = m_ref[...]
        for c in range(4):
            block = own_ref[c] if c < 2 else other_ref[c - 2]
            scale = block[BLK : BLK + 16].astype(jnp.float32)[0:1]
            delta = (
                jnp.dot(p_ref[c], block[0:BLK], preferred_element_type=jnp.float32) * scale
            )
            at = pl.ds(pl.multiple_of(place_ref[16 + c] * BLK, BLK), BLK)
            total[:, at] += delta
        for q in range(4):
            out_ref[place_ref[4 * i + q]] = total[q * BLK : (q + 1) * BLK, :].astype(jnp.bfloat16)


def shards(
    learn_hidden,
    learn_cotangent,
    master_blocks,
    changed,
    rollout_slot,
    rollout_weight,
    rollout_scale,
    decode_hidden,
    decode_routes,
    decode_gates,
):
    dp_count = lax.axis_size("dp")
    dp_index = lax.axis_index("dp")
    me = lax.axis_index("expert")
    exp_dev, learn_rows, width_ff = learn_hidden.shape[1:]
    width_local = rollout_weight.shape[2]
    per_group = master_blocks.shape[2]
    row_blocks = width_ff // BLK
    tokens = decode_hidden.shape[0] * decode_hidden.shape[1]
    big = pltpu.CompilerParams(vmem_limit_bytes=40 * 1024 * 1024)

    codes = lax.dynamic_index_in_dim(changed, me, 0, keepdims=False).reshape(-1)
    tiles = pl.pallas_call(
        select_kernel,
        out_shape=jax.ShapeDtypeStruct((dp_count, per_group, 2, learn_rows, BLK), jnp.bfloat16),
        in_specs=[smem(), vmem(), vmem()],
        out_specs=vmem(),
        compiler_params=big,
    )(codes, learn_hidden[0], learn_cotangent[0])
    received = lax.all_to_all(tiles, "dp", 0, 0, tiled=True)

    chunk = pl.pallas_call(
        chunk_kernel,
        out_shape=jax.ShapeDtypeStruct((tokens + 16, width_ff), jnp.bfloat16),
        in_specs=[vmem()] * 3,
        out_specs=vmem(),
    )(decode_hidden, decode_routes, decode_gates)
    line = [chunk] + [lax.ppermute(chunk, "expert", line_shift(0, s)) for s in SHIFTS]
    line = jnp.stack(line)
    pieces = [line] + [lax.ppermute(line, "expert", line_shift(1, s)) for s in SHIFTS]

    experts_all = rollout_slot.shape[0]
    chip = me // CORES
    own_first = jnp.arange(CORES * exp_dev, dtype=jnp.int32)
    position = (me ^ (own_first // exp_dev)) * exp_dev + own_first % exp_dev
    expert_of = jnp.sum(
        jnp.where(
            rollout_slot[None, :] == position[:, None],
            jnp.arange(experts_all, dtype=jnp.int32)[None, :],
            0,
        ),
        axis=1,
    )
    here = lax.dynamic_index_in_dim(changed, dp_index, 1, keepdims=False)
    here_expert = jnp.arange(here.shape[0], dtype=jnp.int32)[:, None] * exp_dev + (here >> 4)
    where_hit = (
        (here_expert.reshape(-1) == expert_of[:exp_dev, None, None, None])
        & ((here.reshape(-1) & 15) == (jnp.arange(row_blocks, dtype=jnp.int32)[:, None, None] * 2
                                       + jnp.arange(2, dtype=jnp.int32)[:, None]))
    )
    replaced = jnp.any(where_hit, axis=-1)
    kept = jnp.where(replaced, 0.0, rollout_scale.astype(jnp.float32))
    scale_cols = jnp.repeat(kept, BLK, axis=2)
    own_weight = (
        rollout_weight.reshape(exp_dev, row_blocks, BLK, width_local).astype(jnp.float32)
        * scale_cols[:, :, None, :]
    ).astype(jnp.bfloat16).reshape(exp_dev, width_ff, width_local)
    other_weight = lax.ppermute(own_weight, "expert", core_swap())

    pair = jnp.stack([me, me ^ 1])
    pair_codes = jnp.take(here, pair, axis=0)
    pair_expert = (pair[:, None] * exp_dev + (pair_codes >> 4)).reshape(-1)
    ids = jnp.concatenate([expert_of, pair_expert, ((pair_codes >> 1) & 7).reshape(-1)])

    rows = SIDE * tokens
    parts = [
        pl.pallas_call(
            main_kernel,
            out_shape=(
                jax.ShapeDtypeStruct((rows, width_local), jnp.float32),
                jax.ShapeDtypeStruct((4, rows, BLK), jnp.bfloat16),
            ),
            in_specs=[smem(), vmem(), vmem(), vmem()],
            out_specs=(vmem(), vmem()),
            compiler_params=big,
            cost_estimate=pl.CostEstimate(
                flops=2 * rows * width_ff * width_local * 8,
                bytes_accessed=8 * 1024 * 1024,
                transcendentals=0,
            ),
        )(ids, piece, own_weight, other_weight)
        for piece in pieces
    ]

    step_size = learning_rate / math.sqrt(dp_count * learn_rows)
    own_block = pl.pallas_call(
        functools.partial(refresh_kernel, step_size=step_size),
        out_shape=jax.ShapeDtypeStruct((per_group, BLK + 16, BLK), jnp.bfloat16),
        in_specs=[vmem(), vmem()],
        out_specs=vmem(),
    )(received, master_blocks[0, 0])
    other_block = lax.ppermute(own_block, "expert", core_swap())

    x, y, core = chip // SIDE, chip % SIDE, me % CORES
    shifts = jnp.array((0,) + SHIFTS, jnp.int32)
    second, first = shifts[:, None], shifts[None, :]
    from_x = (x + SIDE - jnp.where(core == 0, second, first)) % SIDE
    from_y = (y + SIDE - jnp.where(core == 0, first, second)) % SIDE
    place = jnp.concatenate([(from_x * SIDE + from_y).reshape(-1), (pair_codes & 1).reshape(-1)])
    outgoing = pl.pallas_call(
        combine_kernel,
        out_shape=jax.ShapeDtypeStruct((SIDE * SIDE, tokens, width_local), jnp.bfloat16),
        in_specs=[smem()] + [vmem()] * 10,
        out_specs=vmem(),
        scratch_shapes=[pltpu.VMEM((rows, width_local), jnp.float32)],
        compiler_params=big,
    )(place, own_block, other_block, *[p[0] for p in parts], *[p[1] for p in parts])

    returned = lax.all_to_all(
        outgoing, "expert", 0, 0, axis_index_groups=same_core(), tiled=True
    )
    result = jnp.sum(returned.astype(jnp.float32), axis=0).astype(jnp.bfloat16)
    return result.reshape(decode_hidden.shape[0], decode_hidden.shape[1], width_local)


def solution(mesh):
    return jax.shard_map(
        shards,
        mesh=mesh,
        in_specs=(
            P("dp", "expert", None, None),
            P("dp", "expert", None, None),
            P("expert", "dp", None, None, None),
            P(),
            P(),
            P("expert", None, "dp"),
            P("expert", None, "dp"),
            P(None, "expert", None),
            P(None, "expert", None),
            P(None, "expert", None),
        ),
        out_specs=P(None, "expert", "dp"),
        check_vma=False,
    )
```

time: 251 us -> 116 us (0.46)
  the two profiles are of different devices: /device:TPU:1 before, /device:TPU:32 now
where the time goes in v1:
time: 116 us; the launch traced here: 115 us
  starting transfers between devices  40.1 us (35%)
  Pallas kernels  24.3 us (21%)
  blocking collectives  21.2 us (18%)
  waiting for transfers between devices  17.7 us (15%)
  other arithmetic  7.4 us (6%)
  local copies, waits for them, and re-layouts  4.4 us (4%)
    all_to_all x1, blocking collectives, shards(): lax.all_to_all(outgoing, 'expert', 0, 0, axis_index_groups=same_core(), t...  21.2 us
    pallas_call x4, Pallas kernels, shards(): pl.pallas_call(main_kernel, out_shape=(jax.ShapeDtypeStruct((rows, width_...  17.1 us
    all_to_all x1, starting transfers between devices, shards(): received = lax.all_to_all(tiles, 'dp', 0, 0, tiled=True)  15.2 us
    ppermute x3, waiting for transfers between devices, shards(): lax.ppermute(line, 'expert', line_shift(1, s))  12.1 us
    ppermute x3, starting transfers between devices, shards(): lax.ppermute(chunk, 'expert', line_shift(0, s))  10.9 us
    ppermute x3, starting transfers between devices, shards(): lax.ppermute(line, 'expert', line_shift(1, s))  10.2 us
    ppermute x3, waiting for transfers between devices, shards(): lax.ppermute(chunk, 'expert', line_shift(0, s))  5.61 us
  transfers between devices with their start and end apart: 9, of which 3 were waited for; matrix products, arithmetic and copies ran while one was open for 4% of the time, Pallas kernels for 20%

profile of v1, /device:TPU:32, one launch (start us, length us, event | category | flops | bytes accessed | tf_op | source)
XLA Modules:
  0.0 115.4 jit_solution(6845966121079738824)
XLA Ops:
  1.3 0.8 select_reduce_fusion
  3.3 2.1 %fusion.own_ref = bf16[4,1024,256]{2,1,0:T(8,128)(2,1)S(1)} fusion(bf16[4,1024,256]{2,1,0:T(8,128)(2,1)} %param.16, f32[4,8,256]{2,1,0:T(8,128)S(1)} %broadcast_bitcast_fusion), kind=kLoop, calls=%fused_computation.2 | loop fusion | flops 3145728 | bytes 4227072 | tf_op jit(solution)/shard_map/convert_element_type | solution.py:225
  5.4 1.9 %collective-permute-start.4 = (bf16[4,1024,256]{2,1,0:T(8,128)(2,1)S(1)}, bf16[4,1024,256]{2,1,0:T(8,128)(2,1)}, u32[]{:S(2)}, u32[]{:S(2)}) collective-permute-start(bf16[4,1024,256]{2,1,0:T(8,128)(2,1)S(1)} %fusion.own_ref), channel_id=1, source_target_pairs={{0,1},{1,0},{2,3},{3,2},{4,5},{5,4},{6,7},{7,6},{8,9},{9,8},{10,11... | collective-permute-start | bytes 6291464 | tf_op jit(solution)/shard_map/ppermute | solution.py:226
  7.9 1.5 %shard_map.109 = bf16[16,2,2,32,128]{4,3,2,1,0:T(8,128)(2,1)} custom-call(s32[32]{0:T(128)S(1)} %reshape.273.code_ref, bf16[4,32,1024]{2,1,0:T(8,128)(2,1)S(1)} %bitcast.28, bf16[4,32,4096]{2,1,0:T(8,128)(2,1)S(1)} %bitcast.27), custom_call_target="tpu_custom_call" | custom-call | tf_op jit(solution)/shard_map/pallas_call | solution.py:181
  9.4 15.2 %all-to-all-start = ((bf16[16,2,2,32,128]{4,3,2,1,0:T(8,128)(2,1)}), bf16[16,2,2,32,128]{4,3,2,1,0:T(8,128)(2,1)}, u32[]{:S(2)}, u32[]{:S(2)}) async-start(bf16[16,2,2,32,128]{4,3,2,1,0:T(8,128)(2,1)} %shard_map.109), calls=%async_computation | async-start | bytes 1048576 | tf_op jit(solution)/shard_map/all_to_all | solution.py:188
  26.1 1.9 %shard_map.111 = bf16[144,1024]{1,0:T(8,128)(2,1)} custom-call(bf16[2,64,1024]{2,1,0:T(8,128)(2,1)} %token_ref.1, s32[2,64,8]{2,1,0:T(8,128)} %copy.23.route_ref, f32[2,64,8]{2,1,0:T(8,128)} %copy.24.gate_ref), custom_call_target="tpu_custom_call" | custom-call | tf_op jit(solution)/shard_map/pallas_call | solution.py:190
  28.0 3.5 %collective-permute-start.1 = (bf16[144,1024]{1,0:T(8,128)(2,1)}, bf16[144,1024]{1,0:T(8,128)(2,1)S(1)}, u32[]{:S(2)}, u32[]{:S(2)}) collective-permute-start(bf16[144,1024]{1,0:T(8,128)(2,1)} %shard_map.111), channel_id=1, source_target_pairs={{0,2},{1,9},{2,4},{3,11},{4,6},{5,13},{6,0},{7,15},{8,10},{9,17},{... | collective-permute-start | bytes 884744 | tf_op jit(solution)/shard_map/ppermute | solution.py:196
  31.4 3.6 %collective-permute-start.2 = (bf16[144,1024]{1,0:T(8,128)(2,1)}, bf16[144,1024]{1,0:T(8,128)(2,1)S(1)}, u32[]{:S(2)}, u32[]{:S(2)}) collective-permute-start(bf16[144,1024]{1,0:T(8,128)(2,1)} %shard_map.111), channel_id=1, source_target_pairs={{0,6},{1,25},{2,0},{3,27},{4,2},{5,29},{6,4},{7,31},{8,14},{9,1},{... | collective-permute-start | bytes 884744 | tf_op jit(solution)/shard_map/ppermute | solution.py:196
  35.0 3.9 %collective-permute-start.3 = (bf16[144,1024]{1,0:T(8,128)(2,1)}, bf16[144,1024]{1,0:T(8,128)(2,1)S(1)}, u32[]{:S(2)}, u32[]{:S(2)}) collective-permute-start(bf16[144,1024]{1,0:T(8,128)(2,1)} %shard_map.111), channel_id=1, source_target_pairs={{0,4},{1,17},{2,6},{3,19},{4,0},{5,21},{6,2},{7,23},{8,12},{9,25},... | collective-permute-start | bytes 884744 | tf_op jit(solution)/shard_map/ppermute | solution.py:196
  40.3 5.1 %collective-permute-done.3 = bf16[144,1024]{1,0:T(8,128)(2,1)S(1)} collective-permute-done((bf16[144,1024]{1,0:T(8,128)(2,1)}, bf16[144,1024]{1,0:T(8,128)(2,1)S(1)}, u32[]{:S(2)}, u32[]{:S(2)}) %collective-permute-start.3) | collective-permute-done | bytes 294944 | tf_op jit(solution)/shard_map/ppermute | solution.py:196
  46.0 1.4 %pad_maximum_fusion.x_ref = bf16[4,144,1024]{2,1,0:T(8,128)(2,1)S(1)} fusion(bf16[1,144,1024]{2,1,0:T(8,128)(2,1)} %bitcast.32, bf16[1,144,1024]{2,1,0:T(8,128)(2,1)} %bitcast.31, bf16[1,144,1024]{2,1,0:T(8,128)(2,1)} %bitcast.30, bf16[1,144,1024]{2,1,0:T(8,128)(2,1)} %bitcast.29), kind=kLoop, calls=%fused_computation.3 | loop fusion | flops 1769472 | bytes 2359296 | tf_op jit(solution)/shard_map/stack | solution.py:197
  47.4 4.7 %collective-permute-start.6 = (bf16[4,144,1024]{2,1,0:T(8,128)(2,1)S(1)}, bf16[4,144,1024]{2,1,0:T(8,128)(2,1)}, u32[]{:S(2)}, u32[]{:S(2)}) collective-permute-start(bf16[4,144,1024]{2,1,0:T(8,128)(2,1)S(1)} %pad_maximum_fusion.x_ref), channel_id=1, source_target_pairs={{0,24},{1,7},{2,26},{3,1},{4,28},{5,3},{6,30},{7,5},{8,0},{9,15},{... | collective-permute-start | bytes 3538952 | tf_op jit(solution)/shard_map/ppermute | solution.py:198
  52.2 2.7 %collective-permute-start.7 = (bf16[4,144,1024]{2,1,0:T(8,128)(2,1)S(1)}, bf16[4,144,1024]{2,1,0:T(8,128)(2,1)}, u32[]{:S(2)}, u32[]{:S(2)}) collective-permute-start(bf16[4,144,1024]{2,1,0:T(8,128)(2,1)S(1)} %pad_maximum_fusion.x_ref), channel_id=1, source_target_pairs={{0,16},{1,5},{2,18},{3,7},{4,20},{5,1},{6,22},{7,3},{8,24},{9,13},... | collective-permute-start | bytes 3538952 | tf_op jit(solution)/shard_map/ppermute | solution.py:198
  55.1 2.8 %collective-permute-start.5 = (bf16[4,144,1024]{2,1,0:T(8,128)(2,1)S(1)}, bf16[4,144,1024]{2,1,0:T(8,128)(2,1)}, u32[]{:S(2)}, u32[]{:S(2)}) collective-permute-start(bf16[4,144,1024]{2,1,0:T(8,128)(2,1)S(1)} %pad_maximum_fusion.x_ref), channel_id=1, source_target_pairs={{0,8},{1,3},{2,10},{3,5},{4,12},{5,7},{6,14},{7,1},{8,16},{9,11},{... | collective-permute-start | bytes 3538952 | tf_op jit(solution)/shard_map/ppermute | solution.py:198
  58.4 2.1 %shard_map.110.own_ref = bf16[2,144,128]{2,1,0:T(8,128)(2,1)} custom-call(bf16[16,2,2,32,128]{4,3,2,1,0:T(8,128)(2,1)} %all-to-all-done.recv_ref, f32[2,128,128]{2,1,0:T(8,128)} %bitcast.33), custom_call_target="tpu_custom_call" | custom-call | tf_op jit(solution)/shard_map/pallas_call | solution.py:254
  60.5 1.9 %collective-permute-start = (bf16[2,144,128]{2,1,0:T(8,128)(2,1)}, bf16[2,144,128]{2,1,0:T(8,128)(2,1)S(1)}, u32[]{:S(2)}, u32[]{:S(2)}) collective-permute-start(bf16[2,144,128]{2,1,0:T(8,128)(2,1)} %shard_map.110.own_ref), channel_id=1, source_target_pairs={{0,1},{1,0},{2,3},{3,2},{4,5},{5,4},{6,7},{7,6},{8,9},{9,8},{10,11... | collective-permute-start | bytes 221192 | tf_op jit(solution)/shard_map/ppermute | solution.py:260
  62.4 4.0 %shard_map.112 = (f32[512,256]{1,0:T(8,128)S(1)}, bf16[4,512,128]{2,1,0:T(8,128)(2,1)S(1)}) custom-call(s32[16]{0:T(128)S(1)} %pad_add_fusion.2.id_ref, bf16[4,144,1024]{2,1,0:T(8,128)(2,1)S(1)} %pad_maximum_fusion.x_ref, bf16[4,1024,256]{2,1,0:T(8,128)(2,1)S(1)} %fusion.own_ref, bf16[4,1024,256]{2,1,0:T(8,128)(2,1)} %collective-permute-done.4.other_ref), custom_call_target="tpu_custom_call" | custom-call | flops 2147483648 | bytes 8388608 | tf_op jit(solution)/shard_map/pallas_call | solution.py:235
  66.4 12.0 %collective-permute-done.6.x_ref = bf16[4,144,1024]{2,1,0:T(8,128)(2,1)} collective-permute-done((bf16[4,144,1024]{2,1,0:T(8,128)(2,1)S(1)}, bf16[4,144,1024]{2,1,0:T(8,128)(2,1)}, u32[]{:S(2)}, u32[]{:S(2)}) %collective-permute-start.6) | collective-permute-done | bytes 1179680 | tf_op jit(solution)/shard_map/ppermute | solution.py:198
  78.5 4.4 %shard_map.114 = (f32[512,256]{1,0:T(8,128)S(1)}, bf16[4,512,128]{2,1,0:T(8,128)(2,1)S(1)}) custom-call(s32[16]{0:T(128)S(1)} %pad_add_fusion.2.id_ref, bf16[4,144,1024]{2,1,0:T(8,128)(2,1)} %collective-permute-done.6.x_ref, bf16[4,1024,256]{2,1,0:T(8,128)(2,1)S(1)} %fusion.own_ref, bf16[4,1024,256]{2,1,0:T(8,128)(2,1)} %collective-permute-done.4.other_ref), custom_call_target="tpu_custom_call" | custom-call | flops 2147483648 | bytes 8388608 | tf_op jit(solution)/shard_map/pallas_call | solution.py:235
  82.9 4.4 %shard_map.115 = (f32[512,256]{1,0:T(8,128)S(1)}, bf16[4,512,128]{2,1,0:T(8,128)(2,1)S(1)}) custom-call(s32[16]{0:T(128)S(1)} %pad_add_fusion.2.id_ref, bf16[4,144,1024]{2,1,0:T(8,128)(2,1)} %collective-permute-done.7.x_ref, bf16[4,1024,256]{2,1,0:T(8,128)(2,1)S(1)} %fusion.own_ref, bf16[4,1024,256]{2,1,0:T(8,128)(2,1)} %collective-permute-done.4.other_ref), custom_call_target="tpu_custom_call" | custom-call | flops 2147483648 | bytes 8388608 | tf_op jit(solution)/shard_map/pallas_call | solution.py:235
  87.3 4.4 %shard_map.113 = (f32[512,256]{1,0:T(8,128)S(1)}, bf16[4,512,128]{2,1,0:T(8,128)(2,1)S(1)}) custom-call(s32[16]{0:T(128)S(1)} %pad_add_fusion.2.id_ref, bf16[4,144,1024]{2,1,0:T(8,128)(2,1)} %collective-permute-done.5.x_ref, bf16[4,1024,256]{2,1,0:T(8,128)(2,1)S(1)} %fusion.own_ref, bf16[4,1024,256]{2,1,0:T(8,128)(2,1)} %collective-permute-done.4.other_ref), custom_call_target="tpu_custom_call" | custom-call | flops 2147483648 | bytes 8388608 | tf_op jit(solution)/shard_map/pallas_call | solution.py:235
  91.7 1.7 %shard_map.116 = bf16[16,128,256]{2,1,0:T(8,128)(2,1)S(1)} custom-call(s32[20]{0:T(128)S(1)} %pad_add_fusion.1.place_ref, bf16[2,144,128]{2,1,0:T(8,128)(2,1)S(1)} %copy-done.1, bf16[2,144,128]{2,1,0:T(8,128)(2,1)S(1)} %collective-permute-done.other_ref, f32[512,256]{1,0:T(8,128)S(1)} %get-tuple-element.13.m0, f32[512,256]{1,0:T(8,128)S(1)} %get-tuple-element.14.m1, ...), custom_call_target="tpu_custom_call" | custom-call | tf_op jit(solution)/shard_map/pallas_call | solution.py:268
  93.4 21.2 %all_to_all.10 = bf16[16,128,256]{2,1,0:T(8,128)(2,1)S(1)} all-to-all(bf16[16,128,256]{2,1,0:T(8,128)(2,1)S(1)} %shard_map.116), channel_id=1, replica_groups={{0,2,4,6,8,10,12,14,16,18,20,22,24,26,28,30},{1,3,5,7,9,11,13,15,17,19,..., dimensions={0} | all-to-all | bytes 2097152 | tf_op jit(solution)/shard_map/all_to_all | solution.py:277
  114.6 0.8 reduce_sum.22
  (64 shorter events, 7.3 us)
Async XLA Ops:
  3.3 4.0 %copy-start.6 = (s32[32,16,2]{0,2,1:T(2,128)S(1)}, s32[32,16,2]{0,2,1:T(2,128)}, u32[]{:S(2)}) copy-start(s32[32,16,2]{0,2,1:T(2,128)} %param.14) | copy-start | bytes 12292
  3.3 4.5 %copy-start = (bf16[1,4,32,4096]{3,2,1,0:T(8,128)(2,1)S(1)}, bf16[1,4,32,4096]{3,2,1,0:T(8,128)(2,1)}, u32[]{:S(2)}) copy-start(bf16[1,4,32,4096]{3,2,1,0:T(8,128)(2,1)} %param.12) | copy-start | bytes 3145732
  3.3 4.6 %copy-start.2 = (bf16[1,4,32,1024]{3,2,1,0:T(8,128)(2,1)S(1)}, bf16[1,4,32,1024]{3,2,1,0:T(8,128)(2,1)}, u32[]{:S(2)}) copy-start(bf16[1,4,32,1024]{3,2,1,0:T(8,128)(2,1)} %param.11) | copy-start | bytes 786436
  5.4 57.0 %collective-permute-start.4 = (bf16[4,1024,256]{2,1,0:T(8,128)(2,1)S(1)}, bf16[4,1024,256]{2,1,0:T(8,128)(2,1)}, u32[]{:S(2)}, u32[]{:S(2)}) collective-permute-start(bf16[4,1024,256]{2,1,0:T(8,128)(2,1)S(1)} %fusion.own_ref), channel_id=1, source_target_pairs={{0,1},{1,0},{2,3},{3,2},{4,5},{5,4},{6,7},{7,6},{8,9},{9,8},{10,11... | collective-permute-start | bytes 6291464 | tf_op jit(solution)/shard_map/ppermute | solution.py:226
  7.8 16.7 %copy-start.7 = (s32[2,64,8]{1,2,0:T(8,128)S(1)}, s32[2,64,8]{1,2,0:T(8,128)}, u32[]{:S(2)}) copy-start(s32[2,64,8]{1,2,0:T(8,128)} %param.19) | copy-start | bytes 12292
  7.9 17.5 %copy-start.8 = (f32[2,64,8]{1,2,0:T(8,128)S(1)}, f32[2,64,8]{1,2,0:T(8,128)}, u32[]{:S(2)}) copy-start(f32[2,64,8]{1,2,0:T(8,128)} %param.20) | copy-start | bytes 12292
  9.4 49.1 %all-to-all-start = ((bf16[16,2,2,32,128]{4,3,2,1,0:T(8,128)(2,1)}), bf16[16,2,2,32,128]{4,3,2,1,0:T(8,128)(2,1)}, u32[]{:S(2)}, u32[]{:S(2)}) async-start(bf16[16,2,2,32,128]{4,3,2,1,0:T(8,128)(2,1)} %shard_map.109), calls=%async_computation | async-start | bytes 1048576 | tf_op jit(solution)/shard_map/all_to_all | solution.py:188
  28.0 11.8 %collective-permute-start.1 = (bf16[144,1024]{1,0:T(8,128)(2,1)}, bf16[144,1024]{1,0:T(8,128)(2,1)S(1)}, u32[]{:S(2)}, u32[]{:S(2)}) collective-permute-start(bf16[144,1024]{1,0:T(8,128)(2,1)} %shard_map.111), channel_id=1, source_target_pairs={{0,2},{1,9},{2,4},{3,11},{4,6},{5,13},{6,0},{7,15},{8,10},{9,17},{... | collective-permute-start | bytes 884744 | tf_op jit(solution)/shard_map/ppermute | solution.py:196
  31.4 8.8 %collective-permute-start.2 = (bf16[144,1024]{1,0:T(8,128)(2,1)}, bf16[144,1024]{1,0:T(8,128)(2,1)S(1)}, u32[]{:S(2)}, u32[]{:S(2)}) collective-permute-start(bf16[144,1024]{1,0:T(8,128)(2,1)} %shard_map.111), channel_id=1, source_target_pairs={{0,6},{1,25},{2,0},{3,27},{4,2},{5,29},{6,4},{7,31},{8,14},{9,1},{... | collective-permute-start | bytes 884744 | tf_op jit(solution)/shard_map/ppermute | solution.py:196
  35.0 10.3 %collective-permute-start.3 = (bf16[144,1024]{1,0:T(8,128)(2,1)}, bf16[144,1024]{1,0:T(8,128)(2,1)S(1)}, u32[]{:S(2)}, u32[]{:S(2)}) collective-permute-start(bf16[144,1024]{1,0:T(8,128)(2,1)} %shard_map.111), channel_id=1, source_target_pairs={{0,4},{1,17},{2,6},{3,19},{4,0},{5,21},{6,2},{7,23},{8,12},{9,25},... | collective-permute-start | bytes 884744 | tf_op jit(solution)/shard_map/ppermute | solution.py:196
  39.7 5.6 %copy-start.3 = (bf16[144,1024]{1,0:T(8,128)(2,1)}, bf16[144,1024]{1,0:T(8,128)(2,1)S(1)}, u32[]{:S(2)}) copy-start(bf16[144,1024]{1,0:T(8,128)(2,1)S(1)} %collective-permute-done.1) | copy-start | bytes 884740
  40.3 5.1 %copy-start.4 = (bf16[144,1024]{1,0:T(8,128)(2,1)}, bf16[144,1024]{1,0:T(8,128)(2,1)S(1)}, u32[]{:S(2)}) copy-start(bf16[144,1024]{1,0:T(8,128)(2,1)S(1)} %collective-permute-done.2) | copy-start | bytes 884740
  45.3 0.7 copy-start.5
  46.0 11.9 %copy-start.9 = (s32[4]{0:T(128)S(1)}, s32[4]{0:T(128)}, u32[]{:S(2)}) copy-start(s32[4]{0:T(128)} %constant.130.clone) | copy-start | bytes 52
  47.4 31.0 %collective-permute-start.6 = (bf16[4,144,1024]{2,1,0:T(8,128)(2,1)S(1)}, bf16[4,144,1024]{2,1,0:T(8,128)(2,1)}, u32[]{:S(2)}, u32[]{:S(2)}) collective-permute-start(bf16[4,144,1024]{2,1,0:T(8,128)(2,1)S(1)} %pad_maximum_fusion.x_ref), channel_id=1, source_target_pairs={{0,24},{1,7},{2,26},{3,1},{4,28},{5,3},{6,30},{7,5},{8,0},{9,15},{... | collective-permute-start | bytes 3538952 | tf_op jit(solution)/shard_map/ppermute | solution.py:198
  52.2 30.7 %collective-permute-start.7 = (bf16[4,144,1024]{2,1,0:T(8,128)(2,1)S(1)}, bf16[4,144,1024]{2,1,0:T(8,128)(2,1)}, u32[]{:S(2)}, u32[]{:S(2)}) collective-permute-start(bf16[4,144,1024]{2,1,0:T(8,128)(2,1)S(1)} %pad_maximum_fusion.x_ref), channel_id=1, source_target_pairs={{0,16},{1,5},{2,18},{3,7},{4,20},{5,1},{6,22},{7,3},{8,24},{9,13},... | collective-permute-start | bytes 3538952 | tf_op jit(solution)/shard_map/ppermute | solution.py:198
  55.1 32.1 %collective-permute-start.5 = (bf16[4,144,1024]{2,1,0:T(8,128)(2,1)S(1)}, bf16[4,144,1024]{2,1,0:T(8,128)(2,1)}, u32[]{:S(2)}, u32[]{:S(2)}) collective-permute-start(bf16[4,144,1024]{2,1,0:T(8,128)(2,1)S(1)} %pad_maximum_fusion.x_ref), channel_id=1, source_target_pairs={{0,8},{1,3},{2,10},{3,5},{4,12},{5,7},{6,14},{7,1},{8,16},{9,11},{... | collective-permute-start | bytes 3538952 | tf_op jit(solution)/shard_map/ppermute | solution.py:198
  60.5 31.2 %collective-permute-start = (bf16[2,144,128]{2,1,0:T(8,128)(2,1)}, bf16[2,144,128]{2,1,0:T(8,128)(2,1)S(1)}, u32[]{:S(2)}, u32[]{:S(2)}) collective-permute-start(bf16[2,144,128]{2,1,0:T(8,128)(2,1)} %shard_map.110.own_ref), channel_id=1, source_target_pairs={{0,1},{1,0},{2,3},{3,2},{4,5},{5,4},{6,7},{7,6},{8,9},{9,8},{10,11... | collective-permute-start | bytes 221192 | tf_op jit(solution)/shard_map/ppermute | solution.py:260
  87.3 4.4 %copy-start.1 = (bf16[2,144,128]{2,1,0:T(8,128)(2,1)S(1)}, bf16[2,144,128]{2,1,0:T(8,128)(2,1)}, u32[]{:S(2)}) copy-start(bf16[2,144,128]{2,1,0:T(8,128)(2,1)} %shard_map.110.own_ref) | copy-start | bytes 221188

commit v2 on v1

v2 whole, which is shorter than its diff:
```python
import functools
import math

import jax
import jax.numpy as jnp
from jax import lax
from jax.experimental import pallas as pl
from jax.experimental.pallas import tpu as pltpu
from jax.sharding import PartitionSpec as P

learning_rate = 0.03
quant_limit = 448.0
epsilon_value = 1e-06

SIDE = 4
CORES = 2
BLK = 128
EXTRA = 32
TURNS = (0, 1, 3, 2)
ANY = pl.ANY
VMEM = pltpu.VMEM
SMEM = pltpu.SMEM


def vmem():
    return pl.BlockSpec(memory_space=VMEM)


def smem():
    return pl.BlockSpec(memory_space=SMEM)


def shifted(stage, shift):
    pairs = []
    for x in range(SIDE):
        for y in range(SIDE):
            here = (x * SIDE + y) * CORES
            along_x = ((x + shift) % SIDE * SIDE + y) * CORES
            along_y = (x * SIDE + (y + shift) % SIDE) * CORES
            first, second = (along_y, along_x) if stage == 0 else (along_x, along_y)
            pairs += [(here, first), (here + 1, second + 1)]
    return pairs


def core_swap():
    return [(i, i ^ 1) for i in range(SIDE * SIDE * CORES)]


def both_cores():
    return [[CORES * i, CORES * i + 1] for i in range(SIDE * SIDE)]


def same_core():
    return [[2 * i + core for i in range(SIDE * SIDE)] for core in range(CORES)]


def select_kernel(changed_ref, hidden_ref, cotangent_ref, out_ref, sems):
    me = lax.axis_index("expert")
    groups, per_group = out_ref.shape[0], out_ref.shape[1]
    copies = []
    for g in range(groups):
        for c in range(per_group):
            k = changed_ref[g, c, me]
            e = k >> 4
            r = (k >> 1) & 7
            b = (k & 1) + 2 * g
            for i, (ref, block) in enumerate(((hidden_ref, r), (cotangent_ref, b))):
                copy = pltpu.make_async_copy(
                    ref.at[e, :, pl.ds(pl.multiple_of(block * BLK, BLK), BLK)],
                    out_ref.at[g, c, i],
                    sems.at[g, c, i],
                )
                copy.start()
                copies.append(copy)
    for copy in copies:
        copy.wait()


def chunk_kernel(slot_ref, token_ref, route_ref, gate_ref, out_ref):
    steps, per_step, width = token_ref.shape
    tokens = steps * per_step
    blocks = width // BLK
    route = jnp.concatenate([route_ref[s] for s in range(steps)], axis=1)
    place = jnp.zeros_like(route)
    for e in range(slot_ref.shape[0]):
        place = jnp.where(route == e, slot_ref[e], place)
    gate = jnp.concatenate([gate_ref[s] for s in range(steps)], axis=1)
    high = gate.astype(jnp.bfloat16).astype(jnp.float32)
    low = (gate - high).astype(jnp.bfloat16).astype(jnp.float32)
    extra = jnp.concatenate([place.astype(jnp.float32), high, low, jnp.zeros_like(low)], axis=0)
    extra = extra.astype(jnp.bfloat16)
    for r in range(blocks):
        tile = token_ref[:, :, r * BLK : (r + 1) * BLK].reshape(tokens, BLK)
        out_ref[r * BLK : (r + 1) * BLK, :] = tile
    out_ref[blocks * BLK :, :] = extra


def weight_kernel(changed_ref, slot_ref, scale_ref, own_ref, other_ref, out_ref, kept):
    me, g = lax.axis_index("expert"), lax.axis_index("dp")
    chip = me // CORES
    exp_dev = own_ref.shape[0]
    held, per_expert = scale_ref.shape
    for s in range(held):
        for n in range(per_expert):
            kept[s, n] = scale_ref[s, n]
    for j in range(changed_ref.shape[2]):
        for c in range(changed_ref.shape[1]):
            k = changed_ref[g, c, j]
            place = slot_ref[j * exp_dev + (k >> 4)]

            @pl.when(place // held == chip)
            def _():
                kept[place % held, k & 15] = 0.0

    for h, ref in enumerate((own_ref, other_ref)):
        first = ((me + h) % CORES) * exp_dev
        for s in range(exp_dev):
            for n in range(per_expert):
                rows, columns = pl.ds(n // 2 * BLK, BLK), pl.ds(n % 2 * BLK, BLK)
                scaled = ref[s, rows, columns].astype(jnp.float32) * kept[first + s, n]
                out_ref[h * exp_dev + s, rows, columns] = scaled.astype(jnp.bfloat16)


def gate_columns(x_ref, places):
    base = x_ref.shape[1] - EXTRA
    columns = []
    for q in range(x_ref.shape[0]):
        extra = x_ref[q, base : base + EXTRA, :].astype(jnp.float32)
        place = extra[0:8]
        gate = extra[8:16] + extra[16:24]
        rows = [
            jnp.sum(jnp.where(place == p.astype(jnp.float32), gate, 0.0), axis=0, keepdims=True)
            for p in places
        ]
        rows.append(jnp.zeros((16 - len(places), BLK), jnp.float32))
        columns.append(jnp.transpose(jnp.concatenate(rows, axis=0)))
    return jnp.concatenate(columns, axis=0)


def line_sum(changed_ref, slot_ref, block_ref, weight_ref, x_ref, total):
    me, g = lax.axis_index("expert"), lax.axis_index("dp")
    chip = me // CORES
    held = weight_ref.shape[0]
    exp_dev = held // CORES
    rows = x_ref.shape[0] * BLK
    codes = [changed_ref[g, c % 2, chip * CORES + c // 2] for c in range(4)]
    places = [me * exp_dev + e for e in range(exp_dev)]
    places += [(me ^ 1) * exp_dev + e for e in range(exp_dev)]
    places += [slot_ref[(chip * CORES + c // 2) * exp_dev + (codes[c] >> 4)] for c in range(4)]
    columns = gate_columns(x_ref, places)
    x = jnp.concatenate(
        [
            x_ref[:, r * BLK : (r + 1) * BLK, :].reshape(rows, BLK)
            for r in range(weight_ref.shape[1] // BLK)
        ],
        axis=1,
    )
    value = None
    for e in range(held):
        part = jnp.dot(x, weight_ref[e], preferred_element_type=jnp.float32)
        part = part * columns[:, e : e + 1]
        value = part if value is None else value + part
    total[...] = value
    for c in range(4):
        r = (codes[c] >> 1) & 7
        tile = x_ref[:, pl.ds(pl.multiple_of(r * BLK, BLK), BLK), :].reshape(rows, BLK)
        scale = block_ref[c, BLK : BLK + 16, :].astype(jnp.float32)[0:1, 0:1]
        delta = jnp.dot(tile, block_ref[c, 0:BLK, :], preferred_element_type=jnp.float32)
        at = pl.ds(pl.multiple_of((codes[c] & 1) * BLK, BLK), BLK)
        total[:, at] += delta * (scale * columns[:, held + c : held + c + 1])


def line_kernel(changed_ref, slot_ref, block_ref, weight_ref, x_ref, out_ref, total):
    line_sum(changed_ref, slot_ref, block_ref, weight_ref, x_ref, total)
    out_ref[...] = total[...].astype(jnp.bfloat16)


def refresh_kernel(recv_ref, master_ref, out_ref, *, step_size):
    groups, per_group = recv_ref.shape[0], recv_ref.shape[1]
    rows = groups * recv_ref.shape[3]
    for c in range(per_group):
        left = recv_ref[:, c, 0].reshape(rows, BLK)
        right = recv_ref[:, c, 1].reshape(rows, BLK)
        gradient = lax.dot_general(
            left, right, (((0,), (0,)), ((), ())), preferred_element_type=jnp.float32
        )
        updated = master_ref[c] - step_size * gradient
        peak = jnp.max(jnp.max(jnp.abs(updated), axis=0, keepdims=True), axis=1, keepdims=True)
        scale = ((peak + epsilon_value) / quant_limit).astype(jnp.bfloat16)
        scale = jnp.broadcast_to(scale.astype(jnp.float32), (16, BLK))
        out_ref[c, 0:BLK, :] = (updated / scale[0:1, :]).astype(jnp.bfloat16)
        out_ref[c, BLK : BLK + 16, :] = scale.astype(jnp.bfloat16)


def last_kernel(
    changed_ref, slot_ref, block_ref, weight_ref, x_ref, d0, d1, d2, out_ref, total
):
    me = lax.axis_index("expert")
    chip, core = me // CORES, me % CORES
    x, y = chip // SIDE, chip % SIDE
    line_sum(changed_ref, slot_ref, block_ref, weight_ref, x_ref, total)
    for ref, second in zip((d0, d1, d2, total), TURNS):
        for q, first in enumerate(TURNS):
            x_back = jnp.where(core == 0, second, first)
            y_back = jnp.where(core == 0, first, second)
            to = (x + SIDE - x_back) % SIDE * SIDE + (y + SIDE - y_back) % SIDE
            out_ref[to] = ref[q * BLK : (q + 1) * BLK, :].astype(jnp.bfloat16)


def shards(
    learn_hidden,
    learn_cotangent,
    master_blocks,
    changed,
    rollout_slot,
    rollout_weight,
    rollout_scale,
    decode_hidden,
    decode_routes,
    decode_gates,
):
    dp_count = lax.axis_size("dp")
    exp_dev, learn_rows, width_ff = learn_hidden.shape[1:]
    width_local = rollout_weight.shape[2]
    per_group = master_blocks.shape[2]
    tokens = decode_hidden.shape[0] * decode_hidden.shape[1]
    rows = SIDE * tokens
    limit = pltpu.CompilerParams(vmem_limit_bytes=24 * 1024 * 1024)
    table = jnp.transpose(changed, (1, 2, 0))

    tiles = pl.pallas_call(
        select_kernel,
        out_shape=jax.ShapeDtypeStruct((dp_count, per_group, 2, learn_rows, BLK), jnp.bfloat16),
        in_specs=[smem()] + [pl.BlockSpec(memory_space=ANY)] * 2,
        out_specs=vmem(),
        scratch_shapes=[pltpu.SemaphoreType.DMA((dp_count, per_group, 2))],
        compiler_params=limit,
    )(table, learn_hidden[0], learn_cotangent[0])
    tiles, decode_hidden = lax.optimization_barrier((tiles, decode_hidden))
    received = lax.all_to_all(tiles, "dp", 0, 0, tiled=True)

    chunk = pl.pallas_call(
        chunk_kernel,
        out_shape=jax.ShapeDtypeStruct((width_ff + EXTRA, BLK), jnp.bfloat16),
        in_specs=[smem()] + [vmem()] * 3,
        out_specs=vmem(),
        compiler_params=limit,
    )(
        rollout_slot,
        decode_hidden,
        jnp.transpose(decode_routes, (0, 2, 1)),
        jnp.transpose(decode_gates, (0, 2, 1)),
    )
    line = jnp.stack(
        [chunk] + [lax.ppermute(chunk, "expert", shifted(0, turn)) for turn in TURNS[1:]]
    )

    right, left, far = [lax.ppermute(line, "expert", shifted(1, turn)) for turn in TURNS[1:]]

    other_weight = lax.ppermute(rollout_weight, "expert", core_swap())
    line, rollout_scale = lax.optimization_barrier((line, rollout_scale))
    scales = lax.all_gather(
        rollout_scale, "expert", axis_index_groups=both_cores(), tiled=True
    )
    weights = pl.pallas_call(
        weight_kernel,
        out_shape=jax.ShapeDtypeStruct((CORES * exp_dev,) + rollout_weight.shape[1:], jnp.bfloat16),
        in_specs=[smem()] * 3 + [vmem()] * 2,
        out_specs=vmem(),
        scratch_shapes=[pltpu.SMEM((CORES * exp_dev, 16), jnp.float32)],
        compiler_params=limit,
    )(
        table,
        rollout_slot,
        scales.astype(jnp.float32).reshape(CORES * exp_dev, -1),
        rollout_weight,
        other_weight,
    )

    step_size = learning_rate / math.sqrt(dp_count * learn_rows)
    own_block = pl.pallas_call(
        functools.partial(refresh_kernel, step_size=step_size),
        out_shape=jax.ShapeDtypeStruct((per_group, BLK + 16, BLK), jnp.bfloat16),
        in_specs=[vmem(), vmem()],
        out_specs=vmem(),
        compiler_params=limit,
    )(received, master_blocks[0, 0])
    blocks = lax.all_gather(own_block, "expert", axis_index_groups=both_cores(), tiled=True)

    def add_up(kernel, out_shape, piece, *done):
        return pl.pallas_call(
            kernel,
            out_shape=jax.ShapeDtypeStruct(out_shape, jnp.bfloat16),
            in_specs=[smem()] * 2 + [vmem()] * (3 + len(done)),
            out_specs=vmem(),
            scratch_shapes=[pltpu.VMEM((rows, width_local), jnp.float32)],
            compiler_params=limit,
            cost_estimate=pl.CostEstimate(
                flops=2 * rows * width_ff * width_local * 8,
                bytes_accessed=6 * 1024 * 1024,
                transcendentals=0,
            ),
        )(table, rollout_slot, blocks, weights, piece, *done)

    done_line = add_up(line_kernel, (rows, width_local), line)
    right, done_line = lax.optimization_barrier((right, done_line))
    done_right = add_up(line_kernel, (rows, width_local), right)
    left, done_right = lax.optimization_barrier((left, done_right))
    done_left = add_up(line_kernel, (rows, width_local), left)
    far, done_left = lax.optimization_barrier((far, done_left))
    outgoing = add_up(
        last_kernel, (SIDE * SIDE, tokens, width_local), far, done_line, done_right, done_left
    )

    returned = lax.all_to_all(
        outgoing, "expert", 0, 0, axis_index_groups=same_core(), tiled=True
    )
    result = jnp.sum(returned.astype(jnp.float32), axis=0).astype(jnp.bfloat16)
    return result.reshape(decode_hidden.shape[0], decode_hidden.shape[1], width_local)


def solution(mesh):
    return jax.shard_map(
        shards,
        mesh=mesh,
        in_specs=(
            P("dp", "expert", None, None),
            P("dp", "expert", None, None),
            P("expert", "dp", None, None, None),
            P(),
            P(),
            P("expert", None, "dp"),
            P("expert", None, "dp"),
            P(None, "expert", None),
            P(None, "expert", None),
            P(None, "expert", None),
        ),
        out_specs=P(None, "expert", "dp"),
        check_vma=False,
    )
```

time: 116 us -> 105 us (0.905)
  the two profiles are of different devices: /device:TPU:32 before, /device:TPU:1 now
where the time goes in v2:
time: 105 us; the launch traced here: 103 us
  starting transfers between devices  38.4 us (37%)
  blocking collectives  30.6 us (29%)
  Pallas kernels  23 us (22%)
  waiting for transfers between devices  5.56 us (5%)
  local copies, waits for them, and re-layouts  3.07 us (3%)
  other arithmetic  1.89 us (2%)
    all_to_all x1, blocking collectives, shards(): lax.all_to_all(outgoing, 'expert', 0, 0, axis_index_groups=same_core(), t...  24.7 us
    pallas_call x4, Pallas kernels, add_up(): pl.pallas_call(kernel, out_shape=jax.ShapeDtypeStruct(out_shape, jnp.bflo...  16.1 us
    ppermute x3, starting transfers between devices, shards(): lax.ppermute(line, 'expert', shifted(1, turn))  10.1 us
    ppermute x3, starting transfers between devices, shards(): lax.ppermute(chunk, 'expert', shifted(0, turn))  9.93 us
    all_to_all x1, starting transfers between devices, shards(): received = lax.all_to_all(tiles, 'dp', 0, 0, tiled=True)  9.55 us
    ppermute x1, starting transfers between devices, shards(): other_weight = lax.ppermute(rollout_weight, 'expert', core_swap())  8.78 us
    ppermute x3, waiting for transfers between devices, shards(): lax.ppermute(chunk, 'expert', shifted(0, turn))  5.55 us
    all_gather x1, blocking collectives, shards(): lax.all_gather(rollout_scale, 'expert', axis_index_groups=both_cores(), t...  3.85 us
  transfers between devices with their start and end apart: 8, of which 2 were waited for; matrix products, arithmetic and copies ran while one was open for 1% of the time, Pallas kernels for 18%

profile of v2, /device:TPU:1, one launch (start us, length us, event | category | flops | bytes accessed | tf_op | source)
XLA Modules:
  0.0 102.7 jit_solution(6299088394661656359)
XLA Ops:
  0.0 8.8 %collective-permute-start.3 = (bf16[4,1024,256]{2,1,0:T(8,128)(2,1)}, bf16[4,1024,256]{2,1,0:T(8,128)(2,1)}, u32[]{:S(2)}, u32[]{:S(2)}) collective-permute-start(bf16[4,1024,256]{2,1,0:T(8,128)(2,1)} %own_ref.1), channel_id=1, source_target_pairs={{0,1},{1,0},{2,3},{3,2},{4,5},{5,4},{6,7},{7,6},{8,9},{9,8},{10,11... | collective-permute-start | bytes 6291464 | tf_op jit(solution)/shard_map/ppermute | solution.py:260
  8.8 1.2 %copy-done.1 = bf16[1,4,32,4096]{3,2,1,0:T(8,128)(2,1)S(1)} copy-done((bf16[1,4,32,4096]{3,2,1,0:T(8,128)(2,1)S(1)}, bf16[1,4,32,4096]{3,2,1,0:T(8,128)(2,1)}, u32[]{:S(2)}) %copy-start.1) | copy-done | bytes 1048600
  10.0 0.9 copy-done.2
  11.0 0.7 copy-done.5
  11.7 2.8 %shard_map.100 = bf16[16,2,2,32,128]{4,3,2,1,0:T(8,128)(2,1)} custom-call(s32[16,2,32]{2,1,0:T(2,128)S(1)} %bitcast.16, bf16[4,32,1024]{2,1,0:T(8,128)(2,1)S(1)} %bitcast.14, bf16[4,32,4096]{2,1,0:T(8,128)(2,1)S(1)} %bitcast.13), custom_call_target="tpu_custom_call" | custom-call | tf_op jit(solution)/shard_map/pallas_call | solution.py:231
  14.5 9.6 %all-to-all-start = ((bf16[16,2,2,32,128]{4,3,2,1,0:T(8,128)(2,1)}), bf16[16,2,2,32,128]{4,3,2,1,0:T(8,128)(2,1)S(1)}, u32[]{:S(2)}, u32[]{:S(2)}) async-start(bf16[16,2,2,32,128]{4,3,2,1,0:T(8,128)(2,1)} %shard_map.100), calls=%async_computation | async-start | bytes 1048576 | tf_op jit(solution)/shard_map/all_to_all | solution.py:240
  24.1 0.7 shard_map.102
  24.8 3.1 %collective-permute-start = (bf16[1056,128]{1,0:T(8,128)(2,1)S(1)}, bf16[1056,128]{1,0:T(8,128)(2,1)S(1)}, u32[]{:S(2)}, u32[]{:S(2)}) collective-permute-start(bf16[1056,128]{1,0:T(8,128)(2,1)S(1)} %shard_map.102), channel_id=1, source_target_pairs={{0,2},{1,9},{2,4},{3,11},{4,6},{5,13},{6,0},{7,15},{8,10},{9,17},{... | collective-permute-start | bytes 811016 | tf_op jit(solution)/shard_map/ppermute | solution.py:255
  27.9 3.4 %collective-permute-start.1 = (bf16[1056,128]{1,0:T(8,128)(2,1)S(1)}, bf16[1056,128]{1,0:T(8,128)(2,1)S(1)}, u32[]{:S(2)}, u32[]{:S(2)}) collective-permute-start(bf16[1056,128]{1,0:T(8,128)(2,1)S(1)} %shard_map.102), channel_id=1, source_target_pairs={{0,6},{1,25},{2,0},{3,27},{4,2},{5,29},{6,4},{7,31},{8,14},{9,1},{... | collective-permute-start | bytes 811016 | tf_op jit(solution)/shard_map/ppermute | solution.py:255
  31.3 3.4 %collective-permute-start.2 = (bf16[1056,128]{1,0:T(8,128)(2,1)S(1)}, bf16[1056,128]{1,0:T(8,128)(2,1)S(1)}, u32[]{:S(2)}, u32[]{:S(2)}) collective-permute-start(bf16[1056,128]{1,0:T(8,128)(2,1)S(1)} %shard_map.102), channel_id=1, source_target_pairs={{0,4},{1,17},{2,6},{3,19},{4,0},{5,21},{6,2},{7,23},{8,12},{9,25},... | collective-permute-start | bytes 811016 | tf_op jit(solution)/shard_map/ppermute | solution.py:255
  35.4 4.9 %collective-permute-done.2 = bf16[1056,128]{1,0:T(8,128)(2,1)S(1)} collective-permute-done((bf16[1056,128]{1,0:T(8,128)(2,1)S(1)}, bf16[1056,128]{1,0:T(8,128)(2,1)S(1)}, u32[]{:S(2)}, u32[]{:S(2)}) %collective-permute-start.2) | collective-permute-done | bytes 270368 | tf_op jit(solution)/shard_map/ppermute | solution.py:255
  40.3 1.1 %pad_maximum_fusion.x_ref = bf16[4,1056,128]{2,1,0:T(8,128)(2,1)} fusion(bf16[1,1056,128]{2,1,0:T(8,128)(2,1)S(1)} %bitcast.26, bf16[1,1056,128]{2,1,0:T(8,128)(2,1)S(1)} %bitcast.25, bf16[1,1056,128]{2,1,0:T(8,128)(2,1)S(1)} %bitcast.24, bf16[1,1056,128]{2,1,0:T(8,128)(2,1)S(1)} %bitcast.12), kind=kLoop, calls=%fused_computation | loop fusion | flops 1622016 | bytes 2162688 | tf_op jit(solution)/shard_map/stack | solution.py:254
  41.4 3.2 %collective-permute-start.6 = (bf16[4,1056,128]{2,1,0:T(8,128)(2,1)}, bf16[4,1056,128]{2,1,0:T(8,128)(2,1)}, u32[]{:S(2)}, u32[]{:S(2)}) collective-permute-start(bf16[4,1056,128]{2,1,0:T(8,128)(2,1)} %pad_maximum_fusion.x_ref), channel_id=1, source_target_pairs={{0,8},{1,3},{2,10},{3,5},{4,12},{5,7},{6,14},{7,1},{8,16},{9,11},{... | collective-permute-start | bytes 3244040 | tf_op jit(solution)/shard_map/ppermute | solution.py:258
  44.6 3.4 %collective-permute-start.5 = (bf16[4,1056,128]{2,1,0:T(8,128)(2,1)}, bf16[4,1056,128]{2,1,0:T(8,128)(2,1)}, u32[]{:S(2)}, u32[]{:S(2)}) collective-permute-start(bf16[4,1056,128]{2,1,0:T(8,128)(2,1)} %pad_maximum_fusion.x_ref), channel_id=1, source_target_pairs={{0,24},{1,7},{2,26},{3,1},{4,28},{5,3},{6,30},{7,5},{8,0},{9,15},{... | collective-permute-start | bytes 3244040 | tf_op jit(solution)/shard_map/ppermute | solution.py:258
  48.0 3.5 %collective-permute-start.4 = (bf16[4,1056,128]{2,1,0:T(8,128)(2,1)}, bf16[4,1056,128]{2,1,0:T(8,128)(2,1)}, u32[]{:S(2)}, u32[]{:S(2)}) collective-permute-start(bf16[4,1056,128]{2,1,0:T(8,128)(2,1)} %pad_maximum_fusion.x_ref), channel_id=1, source_target_pairs={{0,16},{1,5},{2,18},{3,7},{4,20},{5,1},{6,22},{7,3},{8,24},{9,13},... | collective-permute-start | bytes 3244040 | tf_op jit(solution)/shard_map/ppermute | solution.py:258
  51.6 3.9 %all_gather.7 = bf16[8,8,2]{1,2,0:T(2,128)(2,1)S(1)} all-gather(bf16[4,8,2]{1,2,0:T(2,128)(2,1)S(1)} %copy-done.10), channel_id=1, replica_groups={{0,1},{2,3},{4,5},{6,7},{8,9},{10,11},{12,13},{14,15},{16,17},{18,19},{..., dimensions={0}, use_global_device_ids=true | all-gather | bytes 384 | tf_op jit(solution)/shard_map/all_gather | solution.py:262
  56.0 2.1 %all_gather.6.block_ref = bf16[4,144,128]{2,1,0:T(8,128)(2,1)S(1)} all-gather(bf16[2,144,128]{2,1,0:T(8,128)(2,1)S(1)} %shard_map.101), channel_id=1, replica_groups={{0,1},{2,3},{4,5},{6,7},{8,9},{10,11},{12,13},{14,15},{16,17},{18,19},{..., dimensions={0}, use_global_device_ids=true | all-gather | bytes 221184 | tf_op jit(solution)/shard_map/all_gather | solution.py:288
  58.1 3.1 %shard_map.103.weight_ref = bf16[8,1024,256]{2,1,0:T(8,128)(2,1)S(1)} custom-call(s32[16,2,32]{2,1,0:T(2,128)S(1)} %bitcast.17, s32[128]{0:T(128)S(1)} %copy-done.9, f32[8,16]{1,0:T(8,128)S(1)} %copy.17.scale_ref, bf16[4,1024,256]{2,1,0:T(8,128)(2,1)S(1)} %copy-done, bf16[4,1024,256]{2,1,0:T(8,128)(2,1)} %collective-permute-done.3.other_ref), custom_call_target="tpu_custom_call" | custom-call | tf_op jit(solution)/shard_map/pallas_call | solution.py:265
  61.1 4.0 %shard_map.104.d0 = bf16[512,256]{1,0:T(8,128)(2,1)S(1)} custom-call(s32[16,2,32]{2,1,0:T(2,128)S(1)} %bitcast.18, s32[128]{0:T(128)S(1)} %copy-done.9, bf16[4,144,128]{2,1,0:T(8,128)(2,1)S(1)} %all_gather.6.block_ref, bf16[8,1024,256]{2,1,0:T(8,128)(2,1)S(1)} %shard_map.103.weight_ref, bf16[4,1056,128]{2,1,0:T(8,128)(2,1)} %pad_maximum_fusion.x_ref), custom_call_target="tpu_custom_call" | custom-call | flops 2147483648 | bytes 6291456 | tf_op jit(solution)/shard_map/pallas_call | solution.py:291
  65.2 4.0 %shard_map.105.d1 = bf16[512,256]{1,0:T(8,128)(2,1)S(1)} custom-call(s32[16,2,32]{2,1,0:T(2,128)S(1)} %bitcast.19, s32[128]{0:T(128)S(1)} %copy-done.9, bf16[4,144,128]{2,1,0:T(8,128)(2,1)S(1)} %all_gather.6.block_ref, bf16[8,1024,256]{2,1,0:T(8,128)(2,1)S(1)} %shard_map.103.weight_ref, bf16[4,1056,128]{2,1,0:T(8,128)(2,1)} %collective-permute-done.6.x_ref), custom_call_target="tpu_custom_call" | custom-call | flops 2147483648 | bytes 6291456 | tf_op jit(solution)/shard_map/pallas_call | solution.py:291
  69.2 4.0 %shard_map.106.d2 = bf16[512,256]{1,0:T(8,128)(2,1)S(1)} custom-call(s32[16,2,32]{2,1,0:T(2,128)S(1)} %bitcast.20, s32[128]{0:T(128)S(1)} %copy-done.9, bf16[4,144,128]{2,1,0:T(8,128)(2,1)S(1)} %all_gather.6.block_ref, bf16[8,1024,256]{2,1,0:T(8,128)(2,1)S(1)} %shard_map.103.weight_ref, bf16[4,1056,128]{2,1,0:T(8,128)(2,1)} %collective-permute-done.5.x_ref), custom_call_target="tpu_custom_call" | custom-call | flops 2147483648 | bytes 6291456 | tf_op jit(solution)/shard_map/pallas_call | solution.py:291
  73.2 4.0 %shard_map.107 = bf16[16,128,256]{2,1,0:T(8,128)(2,1)S(1)} custom-call(s32[16,2,32]{2,1,0:T(2,128)S(1)} %bitcast.21, s32[128]{0:T(128)S(1)} %copy-done.9, bf16[4,144,128]{2,1,0:T(8,128)(2,1)S(1)} %all_gather.6.block_ref, bf16[8,1024,256]{2,1,0:T(8,128)(2,1)S(1)} %shard_map.103.weight_ref, bf16[4,1056,128]{2,1,0:T(8,128)(2,1)} %collective-permute-done.4.x_ref, ...), custom_call_target="tpu_custom_call" | custom-call | flops 2147483648 | bytes 6291456 | tf_op jit(solution)/shard_map/pallas_call | solution.py:291
  77.2 24.7 %all_to_all.10 = bf16[16,128,256]{2,1,0:T(8,128)(2,1)S(1)} all-to-all(bf16[16,128,256]{2,1,0:T(8,128)(2,1)S(1)} %shard_map.107), channel_id=1, replica_groups={{0,2,4,6,8,10,12,14,16,18,20,22,24,26,28,30},{1,3,5,7,9,11,13,15,17,19,..., dimensions={0} | all-to-all | bytes 2097152 | tf_op jit(solution)/shard_map/all_to_all | solution.py:315
  101.9 0.8 reduce_sum.12
  (30 shorter events, 1.2 us)
Async XLA Ops:
  0.0 58.0 %collective-permute-start.3 = (bf16[4,1024,256]{2,1,0:T(8,128)(2,1)}, bf16[4,1024,256]{2,1,0:T(8,128)(2,1)}, u32[]{:S(2)}, u32[]{:S(2)}) collective-permute-start(bf16[4,1024,256]{2,1,0:T(8,128)(2,1)} %own_ref.1), channel_id=1, source_target_pairs={{0,1},{1,0},{2,3},{3,2},{4,5},{5,4},{6,7},{7,6},{8,9},{9,8},{10,11... | collective-permute-start | bytes 6291464 | tf_op jit(solution)/shard_map/ppermute | solution.py:260
  8.8 1.2 %copy-start.1 = (bf16[1,4,32,4096]{3,2,1,0:T(8,128)(2,1)S(1)}, bf16[1,4,32,4096]{3,2,1,0:T(8,128)(2,1)}, u32[]{:S(2)}) copy-start(bf16[1,4,32,4096]{3,2,1,0:T(8,128)(2,1)} %param.11) | copy-start | bytes 3145732
  10.0 0.9 copy-start.2
  11.0 0.7 copy-start.5
  11.7 12.4 %copy-start.3 = (bf16[2,64,1024]{2,1,0:T(8,128)(2,1)S(1)}, bf16[2,64,1024]{2,1,0:T(8,128)(2,1)}, u32[]{:S(2)}) copy-start(bf16[2,64,1024]{2,1,0:T(8,128)(2,1)} %token_ref) | copy-start | bytes 786436
  11.7 12.4 %copy-start.7 = (s32[2,64,8]{1,2,0:T(8,128)S(1)}, s32[2,64,8]{1,2,0:T(8,128)}, u32[]{:S(2)}) copy-start(s32[2,64,8]{1,2,0:T(8,128)} %param.18) | copy-start | bytes 12292
  11.7 12.4 %copy-start.8 = (f32[2,64,8]{1,2,0:T(8,128)S(1)}, f32[2,64,8]{1,2,0:T(8,128)}, u32[]{:S(2)}) copy-start(f32[2,64,8]{1,2,0:T(8,128)} %param.19) | copy-start | bytes 12292
  11.7 12.4 %copy-start.9 = (s32[128]{0:T(128)S(1)}, s32[128]{0:T(128)}, u32[]{:S(2)}) copy-start(s32[128]{0:T(128)} %slot_ref.11) | copy-start | bytes 1540
  14.5 41.1 %all-to-all-start = ((bf16[16,2,2,32,128]{4,3,2,1,0:T(8,128)(2,1)}), bf16[16,2,2,32,128]{4,3,2,1,0:T(8,128)(2,1)S(1)}, u32[]{:S(2)}, u32[]{:S(2)}) async-start(bf16[16,2,2,32,128]{4,3,2,1,0:T(8,128)(2,1)} %shard_map.100), calls=%async_computation | async-start | bytes 1048576 | tf_op jit(solution)/shard_map/all_to_all | solution.py:240
  24.1 31.5 %copy-start.4 = (f32[1,1,2,128,128]{4,3,2,1,0:T(8,128)S(1)}, f32[1,1,2,128,128]{4,3,2,1,0:T(8,128)}, u32[]{:S(2)}) copy-start(f32[1,1,2,128,128]{4,3,2,1,0:T(8,128)} %param.12) | copy-start | bytes 393220
  24.8 10.0 %collective-permute-start = (bf16[1056,128]{1,0:T(8,128)(2,1)S(1)}, bf16[1056,128]{1,0:T(8,128)(2,1)S(1)}, u32[]{:S(2)}, u32[]{:S(2)}) collective-permute-start(bf16[1056,128]{1,0:T(8,128)(2,1)S(1)} %shard_map.102), channel_id=1, source_target_pairs={{0,2},{1,9},{2,4},{3,11},{4,6},{5,13},{6,0},{7,15},{8,10},{9,17},{... | collective-permute-start | bytes 811016 | tf_op jit(solution)/shard_map/ppermute | solution.py:255
  27.9 7.5 %collective-permute-start.1 = (bf16[1056,128]{1,0:T(8,128)(2,1)S(1)}, bf16[1056,128]{1,0:T(8,128)(2,1)S(1)}, u32[]{:S(2)}, u32[]{:S(2)}) collective-permute-start(bf16[1056,128]{1,0:T(8,128)(2,1)S(1)} %shard_map.102), channel_id=1, source_target_pairs={{0,6},{1,25},{2,0},{3,27},{4,2},{5,29},{6,4},{7,31},{8,14},{9,1},{... | collective-permute-start | bytes 811016 | tf_op jit(solution)/shard_map/ppermute | solution.py:255
  31.3 9.0 %collective-permute-start.2 = (bf16[1056,128]{1,0:T(8,128)(2,1)S(1)}, bf16[1056,128]{1,0:T(8,128)(2,1)S(1)}, u32[]{:S(2)}, u32[]{:S(2)}) collective-permute-start(bf16[1056,128]{1,0:T(8,128)(2,1)S(1)} %shard_map.102), channel_id=1, source_target_pairs={{0,4},{1,17},{2,6},{3,19},{4,0},{5,21},{6,2},{7,23},{8,12},{9,25},... | collective-permute-start | bytes 811016 | tf_op jit(solution)/shard_map/ppermute | solution.py:255
  40.3 11.2 %copy-start.10 = (bf16[4,8,2]{1,2,0:T(2,128)(2,1)S(1)}, bf16[4,8,2]{1,2,0:T(2,128)(2,1)}, u32[]{:S(2)}) copy-start(bf16[4,8,2]{1,2,0:T(2,128)(2,1)} %param.16) | copy-start | bytes 388
  40.3 17.7 %copy-start = (bf16[4,1024,256]{2,1,0:T(8,128)(2,1)S(1)}, bf16[4,1024,256]{2,1,0:T(8,128)(2,1)}, u32[]{:S(2)}) copy-start(bf16[4,1024,256]{2,1,0:T(8,128)(2,1)} %own_ref.1) | copy-start | bytes 6291460
  40.3 17.7 %copy-start.6 = (s32[32,16,2]{0,2,1:T(2,128)S(1)}, s32[32,16,2]{0,2,1:T(2,128)}, u32[]{:S(2)}) copy-start(s32[32,16,2]{0,2,1:T(2,128)} %param.13) | copy-start | bytes 12292
  41.4 23.7 %collective-permute-start.6 = (bf16[4,1056,128]{2,1,0:T(8,128)(2,1)}, bf16[4,1056,128]{2,1,0:T(8,128)(2,1)}, u32[]{:S(2)}, u32[]{:S(2)}) collective-permute-start(bf16[4,1056,128]{2,1,0:T(8,128)(2,1)} %pad_maximum_fusion.x_ref), channel_id=1, source_target_pairs={{0,8},{1,3},{2,10},{3,5},{4,12},{5,7},{6,14},{7,1},{8,16},{9,11},{... | collective-permute-start | bytes 3244040 | tf_op jit(solution)/shard_map/ppermute | solution.py:258
  44.6 24.5 %collective-permute-start.5 = (bf16[4,1056,128]{2,1,0:T(8,128)(2,1)}, bf16[4,1056,128]{2,1,0:T(8,128)(2,1)}, u32[]{:S(2)}, u32[]{:S(2)}) collective-permute-start(bf16[4,1056,128]{2,1,0:T(8,128)(2,1)} %pad_maximum_fusion.x_ref), channel_id=1, source_target_pairs={{0,24},{1,7},{2,26},{3,1},{4,28},{5,3},{6,30},{7,5},{8,0},{9,15},{... | collective-permute-start | bytes 3244040 | tf_op jit(solution)/shard_map/ppermute | solution.py:258
  48.0 25.2 %collective-permute-start.4 = (bf16[4,1056,128]{2,1,0:T(8,128)(2,1)}, bf16[4,1056,128]{2,1,0:T(8,128)(2,1)}, u32[]{:S(2)}, u32[]{:S(2)}) collective-permute-start(bf16[4,1056,128]{2,1,0:T(8,128)(2,1)} %pad_maximum_fusion.x_ref), channel_id=1, source_target_pairs={{0,16},{1,5},{2,18},{3,7},{4,20},{5,1},{6,22},{7,3},{8,24},{9,13},... | collective-permute-start | bytes 3244040 | tf_op jit(solution)/shard_map/ppermute | solution.py:258

commit v3 on v2

v3 whole, which is shorter than its diff:
```python
import functools
import math

import jax
import jax.numpy as jnp
from jax import lax
from jax.experimental import pallas as pl
from jax.experimental.pallas import tpu as pltpu
from jax.sharding import PartitionSpec as P

learning_rate = 0.03
quant_limit = 448.0
epsilon_value = 1e-06

SIDE = 4
CORES = 2
BLK = 128
EXTRA = 32
TURNS = (0, 1, 3, 2)
ANY = pl.ANY
VMEM = pltpu.VMEM
SMEM = pltpu.SMEM


def vmem():
    return pl.BlockSpec(memory_space=VMEM)


def smem():
    return pl.BlockSpec(memory_space=SMEM)


def shifted(stage, shift):
    pairs = []
    for x in range(SIDE):
        for y in range(SIDE):
            here = (x * SIDE + y) * CORES
            along_x = ((x + shift) % SIDE * SIDE + y) * CORES
            along_y = (x * SIDE + (y + shift) % SIDE) * CORES
            first, second = (along_y, along_x) if stage == 0 else (along_x, along_y)
            pairs += [(here, first), (here + 1, second + 1)]
    return pairs


def core_swap():
    return [(i, i ^ 1) for i in range(SIDE * SIDE * CORES)]


def both_cores():
    return [[CORES * i, CORES * i + 1] for i in range(SIDE * SIDE)]


def same_core():
    return [[2 * i + core for i in range(SIDE * SIDE)] for core in range(CORES)]


def select_kernel(changed_ref, hidden_hbm, cotangent_hbm, out_ref, hidden_ref, cotangent_ref, sems):
    me = lax.axis_index("expert")
    groups, per_group = out_ref.shape[0], out_ref.shape[1]
    first = pltpu.make_async_copy(hidden_hbm, hidden_ref, sems.at[0])
    second = pltpu.make_async_copy(cotangent_hbm, cotangent_ref, sems.at[1])
    first.start()
    second.start()
    first.wait()
    second.wait()
    for g in range(groups):
        for c in range(per_group):
            k = changed_ref[g, c, me]
            e = k >> 4
            r = (k >> 1) & 7
            b = (k & 1) + 2 * g
            out_ref[g, c, 0] = hidden_ref[e, :, pl.ds(pl.multiple_of(r * BLK, BLK), BLK)]
            out_ref[g, c, 1] = cotangent_ref[e, :, pl.ds(pl.multiple_of(b * BLK, BLK), BLK)]


def chunk_kernel(slot_ref, token_hbm, route_hbm, gate_hbm, out_ref, token_ref, route_ref, gate_ref, sems):
    pairs = ((route_hbm, route_ref), (gate_hbm, gate_ref), (token_hbm, token_ref))
    copies = [pltpu.make_async_copy(a, b, sems.at[n]) for n, (a, b) in enumerate(pairs)]
    for copy in copies:
        copy.start()
    for copy in copies:
        copy.wait()
    steps, per_step, width = token_ref.shape
    tokens = steps * per_step
    blocks = width // BLK
    route = jnp.concatenate([route_ref[s] for s in range(steps)], axis=1)
    place = jnp.zeros_like(route)
    for e in range(slot_ref.shape[0]):
        place = jnp.where(route == e, slot_ref[e], place)
    gate = jnp.concatenate([gate_ref[s] for s in range(steps)], axis=1)
    high = gate.astype(jnp.bfloat16).astype(jnp.float32)
    low = (gate - high).astype(jnp.bfloat16).astype(jnp.float32)
    extra = jnp.concatenate([place.astype(jnp.float32), high, low, jnp.zeros_like(low)], axis=0)
    extra = extra.astype(jnp.bfloat16)
    for r in range(blocks):
        tile = token_ref[:, :, r * BLK : (r + 1) * BLK].reshape(tokens, BLK)
        out_ref[r * BLK : (r + 1) * BLK, :] = tile
    out_ref[blocks * BLK :, :] = extra


def gate_columns(x_ref, places):
    base = x_ref.shape[1] - EXTRA
    columns = []
    for q in range(x_ref.shape[0]):
        extra = x_ref[q, base : base + EXTRA, :].astype(jnp.float32)
        place = extra[0:8]
        gate = extra[8:16] + extra[16:24]
        rows = [
            jnp.sum(jnp.where(place == p.astype(jnp.float32), gate, 0.0), axis=0, keepdims=True)
            for p in places
        ]
        rows.append(jnp.zeros((16 - len(places), BLK), jnp.float32))
        columns.append(jnp.transpose(jnp.concatenate(rows, axis=0)))
    return jnp.concatenate(columns, axis=0)


def chip_blocks(changed_ref, slot_ref, exp_dev):
    me, g = lax.axis_index("expert"), lax.axis_index("dp")
    learners = [me // CORES * CORES + c // 2 for c in range(4)]
    codes = [changed_ref[g, c % 2, learners[c]] for c in range(4)]
    return codes, [slot_ref[j * exp_dev + (k >> 4)] for j, k in zip(learners, codes)]


def kept_scales(changed_ref, slot_ref, scale_ref, kept, exp_dev):
    me, g = lax.axis_index("expert"), lax.axis_index("dp")
    chip = me // CORES
    held, per_expert = scale_ref.shape
    for s in range(held):
        for n in range(per_expert):
            kept[s, n] = scale_ref[s, n]
    for j in range(changed_ref.shape[2]):
        for c in range(changed_ref.shape[1]):
            k = changed_ref[g, c, j]
            place = slot_ref[j * exp_dev + (k >> 4)]

            @pl.when(place // held == chip)
            def _():
                kept[place % held, k & 15] = 0.0


def add_lines(changed_ref, slot_ref, exp_dev, lines, weight_of, sum_ref, picked_ref):
    me = lax.axis_index("expert")
    held = CORES * exp_dev
    codes, block_places = chip_blocks(changed_ref, slot_ref, exp_dev)
    places = [me * exp_dev + e for e in range(exp_dev)]
    places += [(me ^ 1) * exp_dev + e for e in range(exp_dev)]
    columns = jnp.concatenate([gate_columns(x, places + block_places) for x in lines], axis=0)
    rows = SIDE * BLK
    blocks = (lines[0].shape[1] - EXTRA) // BLK

    def tiles(at):
        return jnp.concatenate([x[:, at, :].reshape(rows, BLK) for x in lines], axis=0)

    x = jnp.concatenate([tiles(pl.ds(r * BLK, BLK)) for r in range(blocks)], axis=1)
    value = None
    for e in range(held):
        part = jnp.dot(x, weight_of(e), preferred_element_type=jnp.float32)
        part = part * columns[:, e : e + 1]
        value = part if value is None else value + part
    sum_ref[...] = value.astype(sum_ref.dtype)
    for c in range(4):
        r = (codes[c] >> 1) & 7
        tile = tiles(pl.ds(pl.multiple_of(r * BLK, BLK), BLK))
        gated = tile.astype(jnp.float32) * columns[:, held + c : held + c + 1]
        picked_ref[:, c * BLK : (c + 1) * BLK] = gated.astype(jnp.bfloat16)


def first_kernel(
    changed_ref, slot_ref, scale_ref, own_ref, other_ref, x0, x1, weight_ref, sum_ref, picked_ref, kept
):
    me = lax.axis_index("expert")
    exp_dev = own_ref.shape[0]
    kept_scales(changed_ref, slot_ref, scale_ref, kept, exp_dev)

    def weight_of(e):
        ref = own_ref if e < exp_dev else other_ref
        place = (me + e // exp_dev) % CORES * exp_dev + e % exp_dev
        for n in range(scale_ref.shape[1]):
            rows, columns = pl.ds(n // 2 * BLK, BLK), pl.ds(n % 2 * BLK, BLK)
            scaled = ref[e % exp_dev, rows, columns].astype(jnp.float32) * kept[place, n]
            weight_ref[e, rows, columns] = scaled.astype(jnp.bfloat16)
        return weight_ref[e]

    add_lines(changed_ref, slot_ref, exp_dev, (x0, x1), weight_of, sum_ref, picked_ref)


def second_kernel(changed_ref, slot_ref, weight_ref, x2, x3, sum_ref, picked_ref):
    exp_dev = weight_ref.shape[0] // CORES
    weight_of = lambda e: weight_ref[e]
    add_lines(changed_ref, slot_ref, exp_dev, (x2, x3), weight_of, sum_ref, picked_ref)


def refresh_kernel(recv_ref, master_ref, out_ref, *, step_size):
    groups, per_group = recv_ref.shape[0], recv_ref.shape[1]
    rows = groups * recv_ref.shape[3]
    for c in range(per_group):
        left = recv_ref[:, c, 0].reshape(rows, BLK)
        right = recv_ref[:, c, 1].reshape(rows, BLK)
        gradient = lax.dot_general(
            left, right, (((0,), (0,)), ((), ())), preferred_element_type=jnp.float32
        )
        updated = master_ref[c] - step_size * gradient
        peak = jnp.max(jnp.max(jnp.abs(updated), axis=0, keepdims=True), axis=1, keepdims=True)
        scale = ((peak + epsilon_value) / quant_limit).astype(jnp.bfloat16)
        scale = jnp.broadcast_to(scale.astype(jnp.float32), (16, BLK))
        out_ref[c, 0:BLK, :] = (updated / scale[0:1, :]).astype(jnp.bfloat16)
        out_ref[c, BLK : BLK + 16, :] = scale.astype(jnp.bfloat16)


def last_kernel(changed_ref, slot_ref, block_ref, s0, s1, p0, p1, out_ref, spread):
    me = lax.axis_index("expert")
    chip, core = me // CORES, me % CORES
    x, y = chip // SIDE, chip % SIDE
    codes, _ = chip_blocks(changed_ref, slot_ref, 4)
    spread[...] = jnp.zeros(spread.shape, spread.dtype)
    for c in range(4):
        scale = block_ref[c, BLK : BLK + 16, :].astype(jnp.float32)[0:1]
        at = pl.ds(pl.multiple_of((codes[c] & 1) * BLK, BLK), BLK)
        value = block_ref[c, 0:BLK, :].astype(jnp.float32) * scale
        spread[c * BLK : (c + 1) * BLK, at] = value.astype(jnp.bfloat16)
    for half, (sum_ref, picked_ref) in enumerate(((s0, p0), (s1, p1))):
        delta = jnp.dot(picked_ref[...], spread[...], preferred_element_type=jnp.float32)
        total = (sum_ref[...].astype(jnp.float32) + delta).astype(jnp.bfloat16)
        for n in range(2 * SIDE):
            second, first = TURNS[2 * half + n // SIDE], TURNS[n % SIDE]
            x_back = jnp.where(core == 0, second, first)
            y_back = jnp.where(core == 0, first, second)
            to = (x + SIDE - x_back) % SIDE * SIDE + (y + SIDE - y_back) % SIDE
            out_ref[to] = total[n * BLK : (n + 1) * BLK, :]


def shards(
    learn_hidden,
    learn_cotangent,
    master_blocks,
    changed,
    rollout_slot,
    rollout_weight,
    rollout_scale,
    decode_hidden,
    decode_routes,
    decode_gates,
):
    dp_count = lax.axis_size("dp")
    exp_dev, learn_rows, width_ff = learn_hidden.shape[1:]
    width_local = rollout_weight.shape[2]
    per_group = master_blocks.shape[2]
    tokens = decode_hidden.shape[0] * decode_hidden.shape[1]
    rows = SIDE * tokens
    limit = pltpu.CompilerParams(vmem_limit_bytes=32 * 1024 * 1024)
    whole = pltpu.CompilerParams(vmem_limit_bytes=60 * 1024 * 1024)
    table = jnp.transpose(changed, (1, 2, 0))

    token_args = (
        decode_hidden,
        jnp.transpose(decode_routes, (0, 2, 1)),
        jnp.transpose(decode_gates, (0, 2, 1)),
    )
    chunk = pl.pallas_call(
        chunk_kernel,
        out_shape=jax.ShapeDtypeStruct((width_ff + EXTRA, BLK), jnp.bfloat16),
        in_specs=[smem()] + [pl.BlockSpec(memory_space=ANY)] * 3,
        out_specs=vmem(),
        scratch_shapes=[pltpu.VMEM(a.shape, a.dtype) for a in token_args]
        + [pltpu.SemaphoreType.DMA((3,))],
        compiler_params=whole,
    )(rollout_slot, *token_args)
    chunk, learn_hidden, learn_cotangent, rollout_weight = lax.optimization_barrier(
        (chunk, learn_hidden, learn_cotangent, rollout_weight)
    )
    line = jnp.stack(
        [chunk] + [lax.ppermute(chunk, "expert", shifted(0, turn)) for turn in TURNS[1:]]
    )

    tiles = pl.pallas_call(
        select_kernel,
        out_shape=jax.ShapeDtypeStruct((dp_count, per_group, 2, learn_rows, BLK), jnp.bfloat16),
        in_specs=[smem()] + [pl.BlockSpec(memory_space=ANY)] * 2,
        out_specs=vmem(),
        scratch_shapes=[
            pltpu.VMEM(learn_hidden.shape[1:], jnp.bfloat16),
            pltpu.VMEM(learn_cotangent.shape[1:], jnp.bfloat16),
            pltpu.SemaphoreType.DMA((2,)),
        ],
        compiler_params=whole,
    )(table, learn_hidden[0], learn_cotangent[0])
    line, tiles = lax.optimization_barrier((line, tiles))
    received = lax.all_to_all(tiles, "dp", 0, 0, tiled=True)

    right = lax.ppermute(line, "expert", shifted(1, 1))
    line, right = lax.optimization_barrier((line, right))
    far = lax.ppermute(right, "expert", shifted(1, 1))
    left = lax.ppermute(line, "expert", shifted(1, -1))

    other_weight = lax.ppermute(rollout_weight, "expert", core_swap())
    line, rollout_scale = lax.optimization_barrier((line, rollout_scale))
    scales = lax.all_gather(
        rollout_scale, "expert", axis_index_groups=both_cores(), tiled=True
    )
    scales = scales.astype(jnp.float32).reshape(CORES * exp_dev, -1)

    cost = pl.CostEstimate(
        flops=2 * 2 * rows * width_ff * width_local * 8,
        bytes_accessed=12 * 1024 * 1024,
        transcendentals=0,
    )
    pair_out = (
        jax.ShapeDtypeStruct((2 * rows, width_local), jnp.bfloat16),
        jax.ShapeDtypeStruct((2 * rows, 4 * BLK), jnp.bfloat16),
    )
    held = CORES * exp_dev
    weights, sum_first, picked_first = pl.pallas_call(
        first_kernel,
        out_shape=(jax.ShapeDtypeStruct((held,) + rollout_weight.shape[1:], jnp.bfloat16),)
        + pair_out,
        in_specs=[smem()] * 3 + [vmem()] * 4,
        out_specs=(vmem(),) * 3,
        scratch_shapes=[pltpu.SMEM((held, 16), jnp.float32)],
        compiler_params=limit,
        cost_estimate=cost,
    )(table, rollout_slot, scales, rollout_weight, other_weight, line, right)
    left, far, sum_first = lax.optimization_barrier((left, far, sum_first))
    sum_second, picked_second = pl.pallas_call(
        second_kernel,
        out_shape=pair_out,
        in_specs=[smem()] * 2 + [vmem()] * 3,
        out_specs=(vmem(),) * 2,
        compiler_params=limit,
        cost_estimate=cost,
    )(table, rollout_slot, weights, left, far)
    received, sum_second = lax.optimization_barrier((received, sum_second))

    step_size = learning_rate / math.sqrt(dp_count * learn_rows)
    own_block = pl.pallas_call(
        functools.partial(refresh_kernel, step_size=step_size),
        out_shape=jax.ShapeDtypeStruct((per_group, BLK + 16, BLK), jnp.bfloat16),
        in_specs=[vmem(), vmem()],
        out_specs=vmem(),
        compiler_params=limit,
    )(received, master_blocks[0, 0])
    blocks = lax.all_gather(own_block, "expert", axis_index_groups=both_cores(), tiled=True)

    outgoing = pl.pallas_call(
        last_kernel,
        out_shape=jax.ShapeDtypeStruct((SIDE * SIDE, tokens, width_local), jnp.bfloat16),
        in_specs=[smem()] * 2 + [vmem()] * 5,
        out_specs=vmem(),
        scratch_shapes=[pltpu.VMEM((4 * BLK, width_local), jnp.bfloat16)],
        compiler_params=limit,
    )(table, rollout_slot, blocks, sum_first, sum_second, picked_first, picked_second)

    returned = lax.all_to_all(
        outgoing, "expert", 0, 0, axis_index_groups=same_core(), tiled=True
    )
    result = jnp.sum(returned.astype(jnp.float32), axis=0).astype(jnp.bfloat16)
    return result.reshape(decode_hidden.shape[0], decode_hidden.shape[1], width_local)


def solution(mesh):
    return jax.shard_map(
        shards,
        mesh=mesh,
        in_specs=(
            P("dp", "expert", None, None),
            P("dp", "expert", None, None),
            P("expert", "dp", None, None, None),
            P(),
            P(),
            P("expert", None, "dp"),
            P("expert", None, "dp"),
            P(None, "expert", None),
            P(None, "expert", None),
            P(None, "expert", None),
        ),
        out_specs=P(None, "expert", "dp"),
        check_vma=False,
    )
```

time: 105 us -> 95.7 us (0.911)
  blocking collectives: 30.6 us -> 27.9 us
  waiting for transfers between devices: 5.56 us -> 3.71 us
  Pallas kernels: 23 us -> 21.5 us
  starting transfers between devices: 38.4 us -> 37.1 us
    ppermute x3, waiting for transfers between devices: 5.55 us -> 0.01 us  [shards(): lax.ppermute(chunk, 'expert', shifted(0, turn))]
    all_to_all x1, blocking collectives: 24.7 us -> 19.6 us  [shards(): lax.all_to_all(outgoing, 'expert', 0, 0, axis_index_groups=same_core(), t...]
    pallas_call x5 -> x3, Pallas kernels: 19.1 us -> 15.4 us  [the longest x1 7.66 us: shards(): pl.pallas_call(first_kernel, out_shape=(jax.ShapeDtypeStruct((held,) + ro...]
    ppermute x3, waiting for transfers between devices: 0.01 us -> 3.7 us  [the longest x1 2.33 us: shards(): right = lax.ppermute(line, 'expert', shifted(1, 1))]
    ppermute x1, starting transfers between devices: 8.78 us -> 5.79 us  [shards(): other_weight = lax.ppermute(rollout_weight, 'expert', core_swap())]
    all_to_all x1, starting transfers between devices: 9.55 us -> 12.1 us  [shards(): received = lax.all_to_all(tiles, 'dp', 0, 0, tiled=True)]
    all_gather x1, blocking collectives: 2.09 us -> 3.94 us  [shards(): lax.all_gather(own_block, 'expert', axis_index_groups=both_cores(), tiled...]
    pallas_call x1, Pallas kernels: 0.68 us -> 2.52 us  [shards(): pl.pallas_call(chunk_kernel, out_shape=jax.ShapeDtypeStruct((width_ff + E...]
  transfers between devices with their start and end apart: 8 -> 8, of which waited for: 2 -> 2; matrix products, arithmetic and copies ran while one was open for 1% -> 0% of each run, Pallas kernels for 18% -> 18%
where the time goes in v3:
time: 95.7 us; the launch traced here: 93.9 us
  starting transfers between devices  37.1 us (39%)
  blocking collectives  27.9 us (29%)
  Pallas kernels  21.5 us (22%)
  waiting for transfers between devices  3.71 us (4%)
  local copies, waits for them, and re-layouts  2.56 us (3%)
    all_to_all x1, blocking collectives, shards(): lax.all_to_all(outgoing, 'expert', 0, 0, axis_index_groups=same_core(), t...  19.6 us
    all_to_all x1, starting transfers between devices, shards(): received = lax.all_to_all(tiles, 'dp', 0, 0, tiled=True)  12.1 us
    ppermute x3, starting transfers between devices, shards(): lax.ppermute(chunk, 'expert', shifted(0, turn))  10.9 us
    pallas_call x1, Pallas kernels, shards(): pl.pallas_call(first_kernel, out_shape=(jax.ShapeDtypeStruct((held,) + ro...  7.66 us
    pallas_call x1, Pallas kernels, shards(): pl.pallas_call(second_kernel, out_shape=pair_out, in_specs=[smem()] * 2 +...  6.16 us
    ppermute x1, starting transfers between devices, shards(): other_weight = lax.ppermute(rollout_weight, 'expert', core_swap())  5.79 us
    all_gather x1, blocking collectives, shards(): lax.all_gather(rollout_scale, 'expert', axis_index_groups=both_cores(), t...  4.38 us
    all_gather x1, blocking collectives, shards(): lax.all_gather(own_block, 'expert', axis_index_groups=both_cores(), tiled...  3.94 us
  transfers between devices with their start and end apart: 8, of which 2 were waited for; matrix products, arithmetic and copies ran while one was open for 0% of the time, Pallas kernels for 18%

profile of v3, /device:TPU:1, one launch (start us, length us, event | category | flops | bytes accessed | tf_op | source)
XLA Modules:
  0.0 93.9 jit_solution(14136311182099869504)
XLA Ops:
  0.0 2.5 %shard_map.100 = bf16[1056,128]{1,0:T(8,128)(2,1)} custom-call(s32[128]{0:T(128)} %slot_ref.7, bf16[2,64,1024]{2,1,0:T(8,128)(2,1)} %token_hbm.1, s32[2,8,64]{2,1,0:T(8,128)} %bitcast.24, f32[2,8,64]{2,1,0:T(8,128)} %bitcast.25), custom_call_target="tpu_custom_call" | custom-call | tf_op jit(solution)/shard_map/pallas_call | solution.py:259
  2.5 5.6 %collective-permute-start.2 = (bf16[1056,128]{1,0:T(8,128)(2,1)}, bf16[1056,128]{1,0:T(8,128)(2,1)S(1)}, u32[]{:S(2)}, u32[]{:S(2)}) collective-permute-start(bf16[1056,128]{1,0:T(8,128)(2,1)} %shard_map.100), channel_id=1, source_target_pairs={{0,4},{1,17},{2,6},{3,19},{4,0},{5,21},{6,2},{7,23},{8,12},{9,25},... | collective-permute-start | bytes 811016 | tf_op jit(solution)/shard_map/ppermute | solution.py:272
  8.2 2.8 %collective-permute-start.1 = (bf16[1056,128]{1,0:T(8,128)(2,1)}, bf16[1056,128]{1,0:T(8,128)(2,1)S(1)}, u32[]{:S(2)}, u32[]{:S(2)}) collective-permute-start(bf16[1056,128]{1,0:T(8,128)(2,1)} %shard_map.100), channel_id=1, source_target_pairs={{0,6},{1,25},{2,0},{3,27},{4,2},{5,29},{6,4},{7,31},{8,14},{9,1},{... | collective-permute-start | bytes 811016 | tf_op jit(solution)/shard_map/ppermute | solution.py:272
  10.9 2.5 %collective-permute-start = (bf16[1056,128]{1,0:T(8,128)(2,1)}, bf16[1056,128]{1,0:T(8,128)(2,1)S(1)}, u32[]{:S(2)}, u32[]{:S(2)}) collective-permute-start(bf16[1056,128]{1,0:T(8,128)(2,1)} %shard_map.100), channel_id=1, source_target_pairs={{0,2},{1,9},{2,4},{3,11},{4,6},{5,13},{6,0},{7,15},{8,10},{9,17},{... | collective-permute-start | bytes 811016 | tf_op jit(solution)/shard_map/ppermute | solution.py:272
  13.5 5.8 %collective-permute-start.4 = (bf16[4,1024,256]{2,1,0:T(8,128)(2,1)}, bf16[4,1024,256]{2,1,0:T(8,128)(2,1)}, u32[]{:S(2)}, u32[]{:S(2)}) collective-permute-start(bf16[4,1024,256]{2,1,0:T(8,128)(2,1)} %own_ref), channel_id=1, source_target_pairs={{0,1},{1,0},{2,3},{3,2},{4,5},{5,4},{6,7},{7,6},{8,9},{9,8},{10,11... | collective-permute-start | bytes 6291464 | tf_op jit(solution)/shard_map/ppermute | solution.py:295
  19.3 3.2 %shard_map.101 = bf16[16,2,2,32,128]{4,3,2,1,0:T(8,128)(2,1)} custom-call(s32[16,2,32]{2,1,0:T(2,128)} %bitcast.13, bf16[4,32,1024]{2,1,0:T(8,128)(2,1)} %bitcast.22, bf16[4,32,4096]{2,1,0:T(8,128)(2,1)} %bitcast.18), custom_call_target="tpu_custom_call" | custom-call | tf_op jit(solution)/shard_map/pallas_call | solution.py:275
  22.5 0.1 pad_maximum_fusion.x0
  22.7 3.1 %collective-permute-start.3 = (bf16[4,1056,128]{2,1,0:T(8,128)(2,1)S(1)}, bf16[4,1056,128]{2,1,0:T(8,128)(2,1)}, u32[]{:S(2)}, u32[]{:S(2)}) collective-permute-start(bf16[4,1056,128]{2,1,0:T(8,128)(2,1)S(1)} %pad_maximum_fusion.x0), channel_id=1, source_target_pairs={{0,8},{1,3},{2,10},{3,5},{4,12},{5,7},{6,14},{7,1},{8,16},{9,11},{... | collective-permute-start | bytes 3244040 | tf_op jit(solution)/shard_map/ppermute | solution.py:290
  25.8 12.1 %all-to-all-start = ((bf16[16,2,2,32,128]{4,3,2,1,0:T(8,128)(2,1)}), bf16[16,2,2,32,128]{4,3,2,1,0:T(8,128)(2,1)S(1)}, u32[]{:S(2)}, u32[]{:S(2)}) async-start(bf16[16,2,2,32,128]{4,3,2,1,0:T(8,128)(2,1)} %shard_map.101), calls=%async_computation | async-start | bytes 1048576 | tf_op jit(solution)/shard_map/all_to_all | solution.py:288
  37.9 2.3 %collective-permute-done.3.x1 = bf16[4,1056,128]{2,1,0:T(8,128)(2,1)} collective-permute-done((bf16[4,1056,128]{2,1,0:T(8,128)(2,1)S(1)}, bf16[4,1056,128]{2,1,0:T(8,128)(2,1)}, u32[]{:S(2)}, u32[]{:S(2)}) %collective-permute-start.3) | collective-permute-done | bytes 1081376 | tf_op jit(solution)/shard_map/ppermute | solution.py:290
  40.2 2.8 %collective-permute-start.5 = (bf16[4,1056,128]{2,1,0:T(8,128)(2,1)S(1)}, bf16[4,1056,128]{2,1,0:T(8,128)(2,1)}, u32[]{:S(2)}, u32[]{:S(2)}) collective-permute-start(bf16[4,1056,128]{2,1,0:T(8,128)(2,1)S(1)} %pad_maximum_fusion.x0), channel_id=1, source_target_pairs={{0,24},{1,7},{2,26},{3,1},{4,28},{5,3},{6,30},{7,5},{8,0},{9,15},{... | collective-permute-start | bytes 3244040 | tf_op jit(solution)/shard_map/ppermute | solution.py:293
  43.0 2.5 %collective-permute-start.6 = (bf16[4,1056,128]{2,1,0:T(8,128)(2,1)}, bf16[4,1056,128]{2,1,0:T(8,128)(2,1)}, u32[]{:S(2)}, u32[]{:S(2)}) collective-permute-start(bf16[4,1056,128]{2,1,0:T(8,128)(2,1)} %collective-permute-done.3.x1), channel_id=1, source_target_pairs={{0,8},{1,3},{2,10},{3,5},{4,12},{5,7},{6,14},{7,1},{8,16},{9,11},{... | collective-permute-start | bytes 3244040 | tf_op jit(solution)/shard_map/ppermute | solution.py:292
  45.5 4.4 %all_gather.6 = bf16[8,8,2]{1,2,0:T(2,128)(2,1)S(1)} all-gather(bf16[4,8,2]{1,2,0:T(2,128)(2,1)S(1)} %copy-done.7), channel_id=1, replica_groups={{0,1},{2,3},{4,5},{6,7},{8,9},{10,11},{12,13},{14,15},{16,17},{18,19},{..., dimensions={0}, use_global_device_ids=true | all-gather | bytes 384 | tf_op jit(solution)/shard_map/all_gather | solution.py:297
  49.9 0.1 copy.16
  50.1 1.6 %copy-done.5 = bf16[4,1024,256]{2,1,0:T(8,128)(2,1)S(1)} copy-done((bf16[4,1024,256]{2,1,0:T(8,128)(2,1)S(1)}, bf16[4,1024,256]{2,1,0:T(8,128)(2,1)}, u32[]{:S(2)}) %copy-start.5) | copy-done | bytes 2097176
  51.7 7.7 %shard_map.102 = (bf16[8,1024,256]{2,1,0:T(8,128)(2,1)S(1)}, bf16[1024,256]{1,0:T(8,128)(2,1)S(1)}, bf16[1024,512]{1,0:T(8,128)(2,1)S(1)}) custom-call(s32[16,2,32]{2,1,0:T(2,128)S(1)} %bitcast.14, s32[128]{0:T(128)S(1)} %copy-done.4, f32[8,16]{1,0:T(8,128)S(1)} %copy.17.scale_ref, bf16[4,1024,256]{2,1,0:T(8,128)(2,1)S(1)} %copy-done.5, ...), custom_call_target="tpu_custom_call" | custom-call | flops 4294967296 | bytes 12582912 | tf_op jit(solution)/shard_map/pallas_call | solution.py:312
  59.3 1.4 %collective-permute-done.6.x3 = bf16[4,1056,128]{2,1,0:T(8,128)(2,1)} collective-permute-done((bf16[4,1056,128]{2,1,0:T(8,128)(2,1)}, bf16[4,1056,128]{2,1,0:T(8,128)(2,1)}, u32[]{:S(2)}, u32[]{:S(2)}) %collective-permute-start.6) | collective-permute-done | bytes 1081376 | tf_op jit(solution)/shard_map/ppermute | solution.py:292
  60.7 6.2 %shard_map.103 = (bf16[1024,256]{1,0:T(8,128)(2,1)S(1)}, bf16[1024,512]{1,0:T(8,128)(2,1)S(1)}) custom-call(s32[16,2,32]{2,1,0:T(2,128)S(1)} %bitcast.15, s32[128]{0:T(128)S(1)} %copy-done.4, bf16[8,1024,256]{2,1,0:T(8,128)(2,1)S(1)} %get-tuple-element.35.weight_ref, bf16[4,1056,128]{2,1,0:T(8,128)(2,1)} %collective-permute-done.5.x2, ...), custom_call_target="tpu_custom_call" | custom-call | flops 4294967296 | bytes 12582912 | tf_op jit(solution)/shard_map/pallas_call | solution.py:323
  66.9 0.8 copy-done
  67.7 0.4 shard_map.104
  68.0 3.9 %all_gather.7.block_ref = bf16[4,144,128]{2,1,0:T(8,128)(2,1)S(1)} all-gather(bf16[2,144,128]{2,1,0:T(8,128)(2,1)S(1)} %shard_map.104), channel_id=1, replica_groups={{0,1},{2,3},{4,5},{6,7},{8,9},{10,11},{12,13},{14,15},{16,17},{18,19},{..., dimensions={0}, use_global_device_ids=true | all-gather | bytes 221184 | tf_op jit(solution)/shard_map/all_gather | solution.py:341
  72.0 1.6 %shard_map.105 = bf16[16,128,256]{2,1,0:T(8,128)(2,1)S(1)} custom-call(s32[16,2,32]{2,1,0:T(2,128)S(1)} %bitcast.16, s32[128]{0:T(128)S(1)} %copy-done.4, bf16[4,144,128]{2,1,0:T(8,128)(2,1)S(1)} %all_gather.7.block_ref, bf16[1024,256]{1,0:T(8,128)(2,1)S(1)} %get-tuple-element.41.s0, bf16[1024,256]{1,0:T(8,128)(2,1)S(1)} %copy-done.1, ...), custom_call_target="tpu_custom_call" | custom-call | tf_op jit(solution)/shard_map/pallas_call | solution.py:343
  73.6 19.6 %all_to_all.10 = bf16[16,128,256]{2,1,0:T(8,128)(2,1)S(1)} all-to-all(bf16[16,128,256]{2,1,0:T(8,128)(2,1)S(1)} %shard_map.105), channel_id=1, replica_groups={{0,2,4,6,8,10,12,14,16,18,20,22,24,26,28,30},{1,3,5,7,9,11,13,15,17,19,..., dimensions={0} | all-to-all | bytes 2097152 | tf_op jit(solution)/shard_map/all_to_all | solution.py:352
  93.2 0.8 reduce_sum.12
  (22 shorter events, 0.1 us)
Async XLA Ops:
  2.5 20.0 %copy-start.6 = (bf16[1056,128]{1,0:T(8,128)(2,1)S(1)}, bf16[1056,128]{1,0:T(8,128)(2,1)}, u32[]{:S(2)}) copy-start(bf16[1056,128]{1,0:T(8,128)(2,1)} %shard_map.100) | copy-start | bytes 811012
  2.5 19.9 %collective-permute-start.2 = (bf16[1056,128]{1,0:T(8,128)(2,1)}, bf16[1056,128]{1,0:T(8,128)(2,1)S(1)}, u32[]{:S(2)}, u32[]{:S(2)}) collective-permute-start(bf16[1056,128]{1,0:T(8,128)(2,1)} %shard_map.100), channel_id=1, source_target_pairs={{0,4},{1,17},{2,6},{3,19},{4,0},{5,21},{6,2},{7,23},{8,12},{9,25},... | collective-permute-start | bytes 811016 | tf_op jit(solution)/shard_map/ppermute | solution.py:272
  8.2 14.3 %collective-permute-start.1 = (bf16[1056,128]{1,0:T(8,128)(2,1)}, bf16[1056,128]{1,0:T(8,128)(2,1)S(1)}, u32[]{:S(2)}, u32[]{:S(2)}) collective-permute-start(bf16[1056,128]{1,0:T(8,128)(2,1)} %shard_map.100), channel_id=1, source_target_pairs={{0,6},{1,25},{2,0},{3,27},{4,2},{5,29},{6,4},{7,31},{8,14},{9,1},{... | collective-permute-start | bytes 811016 | tf_op jit(solution)/shard_map/ppermute | solution.py:272
  10.9 11.6 %collective-permute-start = (bf16[1056,128]{1,0:T(8,128)(2,1)}, bf16[1056,128]{1,0:T(8,128)(2,1)S(1)}, u32[]{:S(2)}, u32[]{:S(2)}) collective-permute-start(bf16[1056,128]{1,0:T(8,128)(2,1)} %shard_map.100), channel_id=1, source_target_pairs={{0,2},{1,9},{2,4},{3,11},{4,6},{5,13},{6,0},{7,15},{8,10},{9,17},{... | collective-permute-start | bytes 811016 | tf_op jit(solution)/shard_map/ppermute | solution.py:272
  13.5 36.6 %collective-permute-start.4 = (bf16[4,1024,256]{2,1,0:T(8,128)(2,1)}, bf16[4,1024,256]{2,1,0:T(8,128)(2,1)}, u32[]{:S(2)}, u32[]{:S(2)}) collective-permute-start(bf16[4,1024,256]{2,1,0:T(8,128)(2,1)} %own_ref), channel_id=1, source_target_pairs={{0,1},{1,0},{2,3},{3,2},{4,5},{5,4},{6,7},{7,6},{8,9},{9,8},{10,11... | collective-permute-start | bytes 6291464 | tf_op jit(solution)/shard_map/ppermute | solution.py:295
  22.5 23.0 %copy-start.7 = (bf16[4,8,2]{1,2,0:T(2,128)(2,1)S(1)}, bf16[4,8,2]{1,2,0:T(2,128)(2,1)}, u32[]{:S(2)}) copy-start(bf16[4,8,2]{1,2,0:T(2,128)(2,1)} %param.16) | copy-start | bytes 388
  22.7 27.4 %copy-start.3 = (s32[32,16,2]{0,2,1:T(2,128)S(1)}, s32[32,16,2]{0,2,1:T(2,128)}, u32[]{:S(2)}) copy-start(s32[32,16,2]{0,2,1:T(2,128)} %param.13) | copy-start | bytes 12292
  22.7 27.4 %copy-start.4 = (s32[128]{0:T(128)S(1)}, s32[128]{0:T(128)}, u32[]{:S(2)}) copy-start(s32[128]{0:T(128)} %slot_ref.7) | copy-start | bytes 1540
  22.7 17.5 %collective-permute-start.3 = (bf16[4,1056,128]{2,1,0:T(8,128)(2,1)S(1)}, bf16[4,1056,128]{2,1,0:T(8,128)(2,1)}, u32[]{:S(2)}, u32[]{:S(2)}) collective-permute-start(bf16[4,1056,128]{2,1,0:T(8,128)(2,1)S(1)} %pad_maximum_fusion.x0), channel_id=1, source_target_pairs={{0,8},{1,3},{2,10},{3,5},{4,12},{5,7},{6,14},{7,1},{8,16},{9,11},{... | collective-permute-start | bytes 3244040 | tf_op jit(solution)/shard_map/ppermute | solution.py:290
  25.8 41.9 %all-to-all-start = ((bf16[16,2,2,32,128]{4,3,2,1,0:T(8,128)(2,1)}), bf16[16,2,2,32,128]{4,3,2,1,0:T(8,128)(2,1)S(1)}, u32[]{:S(2)}, u32[]{:S(2)}) async-start(bf16[16,2,2,32,128]{4,3,2,1,0:T(8,128)(2,1)} %shard_map.101), calls=%async_computation | async-start | bytes 1048576 | tf_op jit(solution)/shard_map/all_to_all | solution.py:288
  40.2 19.1 %collective-permute-start.5 = (bf16[4,1056,128]{2,1,0:T(8,128)(2,1)S(1)}, bf16[4,1056,128]{2,1,0:T(8,128)(2,1)}, u32[]{:S(2)}, u32[]{:S(2)}) collective-permute-start(bf16[4,1056,128]{2,1,0:T(8,128)(2,1)S(1)} %pad_maximum_fusion.x0), channel_id=1, source_target_pairs={{0,24},{1,7},{2,26},{3,1},{4,28},{5,3},{6,30},{7,5},{8,0},{9,15},{... | collective-permute-start | bytes 3244040 | tf_op jit(solution)/shard_map/ppermute | solution.py:293
  43.0 17.7 %collective-permute-start.6 = (bf16[4,1056,128]{2,1,0:T(8,128)(2,1)}, bf16[4,1056,128]{2,1,0:T(8,128)(2,1)}, u32[]{:S(2)}, u32[]{:S(2)}) collective-permute-start(bf16[4,1056,128]{2,1,0:T(8,128)(2,1)} %collective-permute-done.3.x1), channel_id=1, source_target_pairs={{0,8},{1,3},{2,10},{3,5},{4,12},{5,7},{6,14},{7,1},{8,16},{9,11},{... | collective-permute-start | bytes 3244040 | tf_op jit(solution)/shard_map/ppermute | solution.py:292
  50.1 1.6 %copy-start.5 = (bf16[4,1024,256]{2,1,0:T(8,128)(2,1)S(1)}, bf16[4,1024,256]{2,1,0:T(8,128)(2,1)}, u32[]{:S(2)}) copy-start(bf16[4,1024,256]{2,1,0:T(8,128)(2,1)} %own_ref) | copy-start | bytes 6291460
  60.7 7.0 %copy-start.2 = (f32[1,1,2,128,128]{4,3,2,1,0:T(8,128)S(1)}, f32[1,1,2,128,128]{4,3,2,1,0:T(8,128)}, u32[]{:S(2)}) copy-start(f32[1,1,2,128,128]{4,3,2,1,0:T(8,128)} %param.12) | copy-start | bytes 393220
  66.9 0.8 copy-start
  67.7 4.3 %copy-start.1 = (bf16[1024,256]{1,0:T(8,128)(2,1)S(1)}, bf16[1024,256]{1,0:T(8,128)(2,1)}, u32[]{:S(2)}) copy-start(bf16[1024,256]{1,0:T(8,128)(2,1)} %copy-done) | copy-start | bytes 1572868

commit v4 on v3

--- a/solution.py
+++ b/solution.py
@@ -40,6 +40,12 @@
             first, second = (along_y, along_x) if stage == 0 else (along_x, along_y)
             pairs += [(here, first), (here + 1, second + 1)]
     return pairs
+
+
+def lines():
+    along_y = [[(x * SIDE + y) * CORES for y in range(SIDE)] for x in range(SIDE)]
+    along_x = [[(x * SIDE + y) * CORES + 1 for x in range(SIDE)] for y in range(SIDE)]
+    return along_y + along_x
 
 
 def core_swap():
@@ -92,10 +98,11 @@
     low = (gate - high).astype(jnp.bfloat16).astype(jnp.float32)
     extra = jnp.concatenate([place.astype(jnp.float32), high, low, jnp.zeros_like(low)], axis=0)
     extra = extra.astype(jnp.bfloat16)
-    for r in range(blocks):
-        tile = token_ref[:, :, r * BLK : (r + 1) * BLK].reshape(tokens, BLK)
-        out_ref[r * BLK : (r + 1) * BLK, :] = tile
-    out_ref[blocks * BLK :, :] = extra
+    for copy in range(out_ref.shape[0]):
+        for r in range(blocks):
+            tile = token_ref[:, :, r * BLK : (r + 1) * BLK].reshape(tokens, BLK)
+            out_ref[copy, r * BLK : (r + 1) * BLK, :] = tile
+        out_ref[copy, blocks * BLK :, :] = extra
 
 
 def gate_columns(x_ref, places):
@@ -132,10 +139,8 @@
         for c in range(changed_ref.shape[1]):
             k = changed_ref[g, c, j]
             place = slot_ref[j * exp_dev + (k >> 4)]
-
-            @pl.when(place // held == chip)
-            def _():
-                kept[place % held, k & 15] = 0.0
+            row = jnp.where(place >> 3 == chip, place & 7, held)
+            kept[row, k & 15] = 0.0
 
 
 def add_lines(changed_ref, slot_ref, exp_dev, lines, weight_of, sum_ref, picked_ref):
@@ -184,10 +189,10 @@
     add_lines(changed_ref, slot_ref, exp_dev, (x0, x1), weight_of, sum_ref, picked_ref)
 
 
-def second_kernel(changed_ref, slot_ref, weight_ref, x2, x3, sum_ref, picked_ref):
+def line_kernel(changed_ref, slot_ref, weight_ref, x_ref, sum_ref, picked_ref):
     exp_dev = weight_ref.shape[0] // CORES
     weight_of = lambda e: weight_ref[e]
-    add_lines(changed_ref, slot_ref, exp_dev, (x2, x3), weight_of, sum_ref, picked_ref)
+    add_lines(changed_ref, slot_ref, exp_dev, (x_ref,), weight_of, sum_ref, picked_ref)
 
 
 def refresh_kernel(recv_ref, master_ref, out_ref, *, step_size):
@@ -207,7 +212,7 @@
         out_ref[c, BLK : BLK + 16, :] = scale.astype(jnp.bfloat16)
 
 
-def last_kernel(changed_ref, slot_ref, block_ref, s0, s1, p0, p1, out_ref, spread):
+def last_kernel(changed_ref, slot_ref, block_ref, s0, s1, s2, p0, p1, p2, out_ref, spread):
     me = lax.axis_index("expert")
     chip, core = me // CORES, me % CORES
     x, y = chip // SIDE, chip % SIDE
@@ -218,14 +223,16 @@
         at = pl.ds(pl.multiple_of((codes[c] & 1) * BLK, BLK), BLK)
         value = block_ref[c, 0:BLK, :].astype(jnp.float32) * scale
         spread[c * BLK : (c + 1) * BLK, at] = value.astype(jnp.bfloat16)
-    for half, (sum_ref, picked_ref) in enumerate(((s0, p0), (s1, p1))):
+    number = 0
+    for sum_ref, picked_ref in ((s0, p0), (s1, p1), (s2, p2)):
         delta = jnp.dot(picked_ref[...], spread[...], preferred_element_type=jnp.float32)
         total = (sum_ref[...].astype(jnp.float32) + delta).astype(jnp.bfloat16)
-        for n in range(2 * SIDE):
-            second, first = TURNS[2 * half + n // SIDE], TURNS[n % SIDE]
-            x_back = jnp.where(core == 0, second, first)
-            y_back = jnp.where(core == 0, first, second)
-            to = (x + SIDE - x_back) % SIDE * SIDE + (y + SIDE - y_back) % SIDE
+        for n in range(sum_ref.shape[0] // BLK):
+            second, first = TURNS[number // SIDE], number % SIDE
+            number += 1
+            along_y = (x + SIDE - second) % SIDE * SIDE + first
+            along_x = first * SIDE + (y + SIDE - second) % SIDE
+            to = jnp.where(core == 0, along_y, along_x)
             out_ref[to] = total[n * BLK : (n + 1) * BLK, :]
 
 
@@ -258,7 +265,7 @@
     )
     chunk = pl.pallas_call(
         chunk_kernel,
-        out_shape=jax.ShapeDtypeStruct((width_ff + EXTRA, BLK), jnp.bfloat16),
+        out_shape=jax.ShapeDtypeStruct((SIDE, width_ff + EXTRA, BLK), jnp.bfloat16),
         in_specs=[smem()] + [pl.BlockSpec(memory_space=ANY)] * 3,
         out_specs=vmem(),
         scratch_shapes=[pltpu.VMEM(a.shape, a.dtype) for a in token_args]
@@ -268,9 +275,7 @@
     chunk, learn_hidden, learn_cotangent, rollout_weight = lax.optimization_barrier(
         (chunk, learn_hidden, learn_cotangent, rollout_weight)
     )
-    line = jnp.stack(
-        [chunk] + [lax.ppermute(chunk, "expert", shifted(0, turn)) for turn in TURNS[1:]]
-    )
+    line = lax.all_to_all(chunk, "expert", 0, 0, axis_index_groups=lines(), tiled=True)
 
     tiles = pl.pallas_call(
         select_kernel,
@@ -299,36 +304,46 @@
     )
     scales = scales.astype(jnp.float32).reshape(CORES * exp_dev, -1)
 
-    cost = pl.CostEstimate(
-        flops=2 * 2 * rows * width_ff * width_local * 8,
-        bytes_accessed=12 * 1024 * 1024,
-        transcendentals=0,
-    )
-    pair_out = (
-        jax.ShapeDtypeStruct((2 * rows, width_local), jnp.bfloat16),
-        jax.ShapeDtypeStruct((2 * rows, 4 * BLK), jnp.bfloat16),
-    )
+    def cost(lines):
+        return pl.CostEstimate(
+            flops=lines * 2 * rows * width_ff * width_local * 8,
+            bytes_accessed=lines * 6 * 1024 * 1024,
+            transcendentals=0,
+        )
+
+    def sums_of(lines):
+        return (
+            jax.ShapeDtypeStruct((lines * rows, width_local), jnp.bfloat16),
+            jax.ShapeDtypeStruct((lines * rows, 4 * BLK), jnp.bfloat16),
+        )
+
     held = CORES * exp_dev
     weights, sum_first, picked_first = pl.pallas_call(
         first_kernel,
         out_shape=(jax.ShapeDtypeStruct((held,) + rollout_weight.shape[1:], jnp.bfloat16),)
-        + pair_out,
+        + sums_of(2),
         in_specs=[smem()] * 3 + [vmem()] * 4,
         out_specs=(vmem(),) * 3,
-        scratch_shapes=[pltpu.SMEM((held, 16), jnp.float32)],
+        scratch_shapes=[pltpu.SMEM((held + 1, 16), jnp.float32)],
         compiler_params=limit,
-        cost_estimate=cost,
+        cost_estimate=cost(2),
     )(table, rollout_slot, scales, rollout_weight, other_weight, line, right)
-    left, far, sum_first = lax.optimization_barrier((left, far, sum_first))
-    sum_second, picked_second = pl.pallas_call(
-        second_kernel,
-        out_shape=pair_out,
-        in_specs=[smem()] * 2 + [vmem()] * 3,
-        out_specs=(vmem(),) * 2,
-        compiler_params=limit,
-        cost_estimate=cost,
-    )(table, rollout_slot, weights, left, far)
-    received, sum_second = lax.optimization_barrier((received, sum_second))
+
+    def add_line(piece):
+        return pl.pallas_call(
+            line_kernel,
+            out_shape=sums_of(1),
+            in_specs=[smem()] * 2 + [vmem()] * 2,
+            out_specs=(vmem(),) * 2,
+            compiler_params=limit,
+            cost_estimate=cost(1),
+        )(table, rollout_slot, weights, piece)
+
+    left, sum_first = lax.optimization_barrier((left, sum_first))
+    sum_left, picked_left = add_line(left)
+    far, sum_left = lax.optimization_barrier((far, sum_left))
+    sum_far, picked_far = add_line(far)
+    received, sum_far = lax.optimization_barrier((received, sum_far))
 
     step_size = learning_rate / math.sqrt(dp_count * learn_rows)
     own_block = pl.pallas_call(
@@ -343,11 +358,14 @@
     outgoing = pl.pallas_call(
         last_kernel,
         out_shape=jax.ShapeDtypeStruct((SIDE * SIDE, tokens, width_local), jnp.bfloat16),
-        in_specs=[smem()] * 2 + [vmem()] * 5,
+        in_specs=[smem()] * 2 + [vmem()] * 7,
         out_specs=vmem(),
         scratch_shapes=[pltpu.VMEM((4 * BLK, width_local), jnp.bfloat16)],
         compiler_params=limit,
-    )(table, rollout_slot, blocks, sum_first, sum_second, picked_first, picked_second)
+    )(
+        table, rollout_slot, blocks,
+        sum_first, sum_left, sum_far, picked_first, picked_left, picked_far,
+    )
 
     returned = lax.all_to_all(
         outgoing, "expert", 0, 0, axis_index_groups=same_core(), tiled=True

time: 95.7 us -> 92.7 us (0.969); the launches traced: 93.9 us -> 92 us
  waiting for transfers between devices: 3.71 us -> 0.61 us
  starting transfers between devices: 37.1 us -> 34.7 us
  Pallas kernels: 21.5 us -> 23.1 us
  blocking collectives: 27.9 us -> 29.2 us
    ppermute x3 -> x0, starting transfers between devices: 10.9 us -> none  [shards(): lax.ppermute(chunk, 'expert', shifted(0, turn))]
    all_to_all x0 -> x1, starting transfers between devices: none -> 4.85 us  [shards(): lax.all_to_all(chunk, 'expert', 0, 0, axis_index_groups=lines(), tiled=True)]
    all_gather x1, blocking collectives: 4.38 us -> 8.33 us  [shards(): lax.all_gather(rollout_scale, 'expert', axis_index_groups=both_cores(), t...]
    all_gather x1, blocking collectives: 3.94 us -> 2.14 us  [shards(): lax.all_gather(own_block, 'expert', axis_index_groups=both_cores(), tiled...]
    ppermute x1, waiting for transfers between devices: 2.33 us -> 0.59 us  [shards(): right = lax.ppermute(line, 'expert', shifted(1, 1))]
    ppermute x1, starting transfers between devices: 5.79 us -> 7.47 us  [shards(): other_weight = lax.ppermute(rollout_weight, 'expert', core_swap())]
    pallas_call x2 -> x3, Pallas kernels: 8.69 us -> 10.3 us  [the longest x2 7.49 us: add_line(): pl.pallas_call(line_kernel, out_shape=sums_of(1), in_specs=[smem()] * 2 +...]
    all_to_all x1, starting transfers between devices: 12.1 us -> 13.5 us  [shards(): received = lax.all_to_all(tiles, 'dp', 0, 0, tiled=True)]
  transfers between devices with their start and end apart: 8 -> 6, of which waited for: 2 -> 1; matrix products, arithmetic and copies ran while one was open for 0% -> 0% of each run, Pallas kernels for 18% -> 20%
where the time goes in v4:
time: 92.7 us; the launch traced here: 92 us
  starting transfers between devices  34.7 us (37%)
  blocking collectives  29.2 us (31%)
  Pallas kernels  23.1 us (25%)
  local copies, waits for them, and re-layouts  3.4 us (4%)
    all_to_all x1, blocking collectives, shards(): lax.all_to_all(outgoing, 'expert', 0, 0, axis_index_groups=same_core(), t...  18.7 us
    all_to_all x1, starting transfers between devices, shards(): received = lax.all_to_all(tiles, 'dp', 0, 0, tiled=True)  13.5 us
    all_gather x1, blocking collectives, shards(): lax.all_gather(rollout_scale, 'expert', axis_index_groups=both_cores(), t...  8.33 us
    pallas_call x2, Pallas kernels, add_line(): pl.pallas_call(line_kernel, out_shape=sums_of(1), in_specs=[smem()] * 2 +...  7.49 us
    ppermute x1, starting transfers between devices, shards(): other_weight = lax.ppermute(rollout_weight, 'expert', core_swap())  7.47 us
    pallas_call x1, Pallas kernels, shards(): pl.pallas_call(first_kernel, out_shape=(jax.ShapeDtypeStruct((held,) + ro...  7.43 us
    all_to_all x1, starting transfers between devices, shards(): lax.all_to_all(chunk, 'expert', 0, 0, axis_index_groups=lines(), tiled=True)  4.85 us
    ppermute x1, starting transfers between devices, shards(): right = lax.ppermute(line, 'expert', shifted(1, 1))  3.6 us
  transfers between devices with their start and end apart: 6, of which 1 were waited for; matrix products, arithmetic and copies ran while one was open for 0% of the time, Pallas kernels for 20%

profile of v4, /device:TPU:1, one launch (start us, length us, event | category | flops | bytes accessed | tf_op | source)
XLA Modules:
  0.0 92.0 jit_solution(15865014059902412891)
XLA Ops:
  0.0 2.8 %shard_map.100 = bf16[4,1056,128]{2,1,0:T(8,128)(2,1)} custom-call(s32[128]{0:T(128)} %slot_ref.9, bf16[2,64,1024]{2,1,0:T(8,128)(2,1)} %token_hbm.1, s32[2,8,64]{2,1,0:T(8,128)} %bitcast.17, f32[2,8,64]{2,1,0:T(8,128)} %bitcast.18), custom_call_target="tpu_custom_call" | custom-call | tf_op jit(solution)/shard_map/pallas_call | solution.py:266
  2.9 4.9 %all-to-all-start = ((bf16[4,1056,128]{2,1,0:T(8,128)(2,1)}), bf16[4,1056,128]{2,1,0:T(8,128)(2,1)S(1)}, u32[]{:S(2)}, u32[]{:S(2)}) async-start(bf16[4,1056,128]{2,1,0:T(8,128)(2,1)} %shard_map.100), calls=%async_computation | async-start | bytes 2162688 | tf_op jit(solution)/shard_map/all_to_all | solution.py:278
  7.7 7.5 %collective-permute-start.1 = (bf16[4,1024,256]{2,1,0:T(8,128)(2,1)}, bf16[4,1024,256]{2,1,0:T(8,128)(2,1)}, u32[]{:S(2)}, u32[]{:S(2)}) collective-permute-start(bf16[4,1024,256]{2,1,0:T(8,128)(2,1)} %own_ref), channel_id=1, source_target_pairs={{0,1},{1,0},{2,3},{3,2},{4,5},{5,4},{6,7},{7,6},{8,9},{9,8},{10,11... | collective-permute-start | bytes 6291464 | tf_op jit(solution)/shard_map/ppermute | solution.py:300
  15.2 0.0 copy-start.4
  15.2 3.4 %shard_map.101 = bf16[16,2,2,32,128]{4,3,2,1,0:T(8,128)(2,1)} custom-call(s32[16,2,32]{2,1,0:T(2,128)} %bitcast.9, bf16[4,32,1024]{2,1,0:T(8,128)(2,1)} %bitcast.15, bf16[4,32,4096]{2,1,0:T(8,128)(2,1)} %bitcast.14), custom_call_target="tpu_custom_call" | custom-call | tf_op jit(solution)/shard_map/pallas_call | solution.py:280
  18.6 3.6 %collective-permute-start = (bf16[4,1056,128]{2,1,0:T(8,128)(2,1)S(1)}, bf16[4,1056,128]{2,1,0:T(8,128)(2,1)}, u32[]{:S(2)}, u32[]{:S(2)}) collective-permute-start(bf16[4,1056,128]{2,1,0:T(8,128)(2,1)S(1)} %all-to-all-done.x0), channel_id=1, source_target_pairs={{0,8},{1,3},{2,10},{3,5},{4,12},{5,7},{6,14},{7,1},{8,16},{9,11},{... | collective-permute-start | bytes 3244040 | tf_op jit(solution)/shard_map/ppermute | solution.py:295
  22.2 13.5 %all-to-all-start.1 = ((bf16[16,2,2,32,128]{4,3,2,1,0:T(8,128)(2,1)}), bf16[16,2,2,32,128]{4,3,2,1,0:T(8,128)(2,1)S(1)}, u32[]{:S(2)}, u32[]{:S(2)}) async-start(bf16[16,2,2,32,128]{4,3,2,1,0:T(8,128)(2,1)} %shard_map.101), calls=%async_computation.1 | async-start | bytes 1048576 | tf_op jit(solution)/shard_map/all_to_all | solution.py:293
  35.8 0.6 collective-permute-done.x1
  36.4 3.4 %collective-permute-start.3 = (bf16[4,1056,128]{2,1,0:T(8,128)(2,1)S(1)}, bf16[4,1056,128]{2,1,0:T(8,128)(2,1)}, u32[]{:S(2)}, u32[]{:S(2)}) collective-permute-start(bf16[4,1056,128]{2,1,0:T(8,128)(2,1)S(1)} %all-to-all-done.x0), channel_id=1, source_target_pairs={{0,24},{1,7},{2,26},{3,1},{4,28},{5,3},{6,30},{7,5},{8,0},{9,15},{... | collective-permute-start | bytes 3244040 | tf_op jit(solution)/shard_map/ppermute | solution.py:298
  39.7 1.9 %collective-permute-start.2 = (bf16[4,1056,128]{2,1,0:T(8,128)(2,1)}, bf16[4,1056,128]{2,1,0:T(8,128)(2,1)}, u32[]{:S(2)}, u32[]{:S(2)}) collective-permute-start(bf16[4,1056,128]{2,1,0:T(8,128)(2,1)} %collective-permute-done.x1), channel_id=1, source_target_pairs={{0,8},{1,3},{2,10},{3,5},{4,12},{5,7},{6,14},{7,1},{8,16},{9,11},{... | collective-permute-start | bytes 3244040 | tf_op jit(solution)/shard_map/ppermute | solution.py:297
  41.7 8.3 %all_gather.6 = bf16[8,8,2]{1,2,0:T(2,128)(2,1)S(1)} all-gather(bf16[4,8,2]{1,2,0:T(2,128)(2,1)S(1)} %copy-done.6), channel_id=1, replica_groups={{0,1},{2,3},{4,5},{6,7},{8,9},{10,11},{12,13},{14,15},{16,17},{18,19},{..., dimensions={0}, use_global_device_ids=true | all-gather | bytes 384 | tf_op jit(solution)/shard_map/all_gather | solution.py:302
  50.0 0.1 copy.16
  50.1 0.1 copy.17.scale_ref
  50.2 1.6 %copy-done.5 = bf16[4,1024,256]{2,1,0:T(8,128)(2,1)S(1)} copy-done((bf16[4,1024,256]{2,1,0:T(8,128)(2,1)S(1)}, bf16[4,1024,256]{2,1,0:T(8,128)(2,1)}, u32[]{:S(2)}) %copy-start.5) | copy-done | bytes 2097176
  51.7 7.4 %shard_map.102 = (bf16[8,1024,256]{2,1,0:T(8,128)(2,1)S(1)}, bf16[1024,256]{1,0:T(8,128)(2,1)S(1)}, bf16[1024,512]{1,0:T(8,128)(2,1)S(1)}) custom-call(s32[16,2,32]{2,1,0:T(2,128)S(1)} %bitcast.10, s32[128]{0:T(128)S(1)} %copy-done.4, f32[8,16]{1,0:T(8,128)S(1)} %copy.17.scale_ref, bf16[4,1024,256]{2,1,0:T(8,128)(2,1)S(1)} %copy-done.5, ...), custom_call_target="tpu_custom_call" | custom-call | flops 4294967296 | bytes 12582912 | tf_op jit(solution)/shard_map/pallas_call | solution.py:321
  59.2 3.7 %shard_map.103 = (bf16[512,256]{1,0:T(8,128)(2,1)S(1)}, bf16[512,512]{1,0:T(8,128)(2,1)S(1)}) custom-call(s32[16,2,32]{2,1,0:T(2,128)S(1)} %bitcast.11, s32[128]{0:T(128)S(1)} %copy-done.4, bf16[8,1024,256]{2,1,0:T(8,128)(2,1)S(1)} %get-tuple-element.38.weight_ref, bf16[4,1056,128]{2,1,0:T(8,128)(2,1)} %collective-permute-done.3.x_ref), custom_call_target="tpu_custom_call" | custom-call | flops 2147483648 | bytes 6291456 | tf_op jit(solution)/shard_map/pallas_call | solution.py:333
  63.0 3.7 %shard_map.104 = (bf16[512,256]{1,0:T(8,128)(2,1)S(1)}, bf16[512,512]{1,0:T(8,128)(2,1)S(1)}) custom-call(s32[16,2,32]{2,1,0:T(2,128)S(1)} %bitcast.12, s32[128]{0:T(128)S(1)} %copy-done.4, bf16[8,1024,256]{2,1,0:T(8,128)(2,1)S(1)} %get-tuple-element.38.weight_ref, bf16[4,1056,128]{2,1,0:T(8,128)(2,1)} %collective-permute-done.2.x_ref), custom_call_target="tpu_custom_call" | custom-call | flops 2147483648 | bytes 6291456 | tf_op jit(solution)/shard_map/pallas_call | solution.py:333
  66.7 0.7 copy-done
  67.4 0.9 %copy-done.2 = f32[1,1,2,128,128]{4,3,2,1,0:T(8,128)S(1)} copy-done((f32[1,1,2,128,128]{4,3,2,1,0:T(8,128)S(1)}, f32[1,1,2,128,128]{4,3,2,1,0:T(8,128)}, u32[]{:S(2)}) %copy-start.2) | copy-done | bytes 131096
  68.4 0.4 shard_map.105
  68.7 2.1 %all_gather.7.block_ref = bf16[4,144,128]{2,1,0:T(8,128)(2,1)S(1)} all-gather(bf16[2,144,128]{2,1,0:T(8,128)(2,1)S(1)} %shard_map.105), channel_id=1, replica_groups={{0,1},{2,3},{4,5},{6,7},{8,9},{10,11},{12,13},{14,15},{16,17},{18,19},{..., dimensions={0}, use_global_device_ids=true | all-gather | bytes 221184 | tf_op jit(solution)/shard_map/all_gather | solution.py:356
  70.9 1.6 %shard_map.106 = bf16[16,128,256]{2,1,0:T(8,128)(2,1)S(1)} custom-call(s32[16,2,32]{2,1,0:T(2,128)S(1)} %bitcast.13, s32[128]{0:T(128)S(1)} %copy-done.4, bf16[4,144,128]{2,1,0:T(8,128)(2,1)S(1)} %all_gather.7.block_ref, bf16[1024,256]{1,0:T(8,128)(2,1)S(1)} %get-tuple-element.45.s0, bf16[512,256]{1,0:T(8,128)(2,1)S(1)} %get-tuple-element.46.s1, ...), custom_call_target="tpu_custom_call" | custom-call | tf_op jit(solution)/shard_map/pallas_call | solution.py:358
  72.5 18.7 %all_to_all.15 = bf16[16,128,256]{2,1,0:T(8,128)(2,1)S(1)} all-to-all(bf16[16,128,256]{2,1,0:T(8,128)(2,1)S(1)} %shard_map.106), channel_id=1, replica_groups={{0,2,4,6,8,10,12,14,16,18,20,22,24,26,28,30},{1,3,5,7,9,11,13,15,17,19,..., dimensions={0} | all-to-all | bytes 2097152 | tf_op jit(solution)/shard_map/all_to_all | solution.py:370
  91.2 0.8 reduce_sum.12
  (16 shorter events, 0.0 us)
Async XLA Ops:
  2.9 15.7 %all-to-all-start = ((bf16[4,1056,128]{2,1,0:T(8,128)(2,1)}), bf16[4,1056,128]{2,1,0:T(8,128)(2,1)S(1)}, u32[]{:S(2)}, u32[]{:S(2)}) async-start(bf16[4,1056,128]{2,1,0:T(8,128)(2,1)} %shard_map.100), calls=%async_computation | async-start | bytes 2162688 | tf_op jit(solution)/shard_map/all_to_all | solution.py:278
  7.7 42.4 %collective-permute-start.1 = (bf16[4,1024,256]{2,1,0:T(8,128)(2,1)}, bf16[4,1024,256]{2,1,0:T(8,128)(2,1)}, u32[]{:S(2)}, u32[]{:S(2)}) collective-permute-start(bf16[4,1024,256]{2,1,0:T(8,128)(2,1)} %own_ref), channel_id=1, source_target_pairs={{0,1},{1,0},{2,3},{3,2},{4,5},{5,4},{6,7},{7,6},{8,9},{9,8},{10,11... | collective-permute-start | bytes 6291464 | tf_op jit(solution)/shard_map/ppermute | solution.py:300
  15.2 26.5 %copy-start.6 = (bf16[4,8,2]{1,2,0:T(2,128)(2,1)S(1)}, bf16[4,8,2]{1,2,0:T(2,128)(2,1)}, u32[]{:S(2)}) copy-start(bf16[4,8,2]{1,2,0:T(2,128)(2,1)} %param.16) | copy-start | bytes 388
  15.2 34.9 %copy-start.3 = (s32[32,16,2]{0,2,1:T(2,128)S(1)}, s32[32,16,2]{0,2,1:T(2,128)}, u32[]{:S(2)}) copy-start(s32[32,16,2]{0,2,1:T(2,128)} %param.13) | copy-start | bytes 12292
  15.2 34.9 %copy-start.4 = (s32[128]{0:T(128)S(1)}, s32[128]{0:T(128)}, u32[]{:S(2)}) copy-start(s32[128]{0:T(128)} %slot_ref.9) | copy-start | bytes 1540
  18.6 17.8 %collective-permute-start = (bf16[4,1056,128]{2,1,0:T(8,128)(2,1)S(1)}, bf16[4,1056,128]{2,1,0:T(8,128)(2,1)}, u32[]{:S(2)}, u32[]{:S(2)}) collective-permute-start(bf16[4,1056,128]{2,1,0:T(8,128)(2,1)S(1)} %all-to-all-done.x0), channel_id=1, source_target_pairs={{0,8},{1,3},{2,10},{3,5},{4,12},{5,7},{6,14},{7,1},{8,16},{9,11},{... | collective-permute-start | bytes 3244040 | tf_op jit(solution)/shard_map/ppermute | solution.py:295
  22.2 45.2 %all-to-all-start.1 = ((bf16[16,2,2,32,128]{4,3,2,1,0:T(8,128)(2,1)}), bf16[16,2,2,32,128]{4,3,2,1,0:T(8,128)(2,1)S(1)}, u32[]{:S(2)}, u32[]{:S(2)}) async-start(bf16[16,2,2,32,128]{4,3,2,1,0:T(8,128)(2,1)} %shard_map.101), calls=%async_computation.1 | async-start | bytes 1048576 | tf_op jit(solution)/shard_map/all_to_all | solution.py:293
  36.4 22.8 %collective-permute-start.3 = (bf16[4,1056,128]{2,1,0:T(8,128)(2,1)S(1)}, bf16[4,1056,128]{2,1,0:T(8,128)(2,1)}, u32[]{:S(2)}, u32[]{:S(2)}) collective-permute-start(bf16[4,1056,128]{2,1,0:T(8,128)(2,1)S(1)} %all-to-all-done.x0), channel_id=1, source_target_pairs={{0,24},{1,7},{2,26},{3,1},{4,28},{5,3},{6,30},{7,5},{8,0},{9,15},{... | collective-permute-start | bytes 3244040 | tf_op jit(solution)/shard_map/ppermute | solution.py:298
  39.7 23.2 %collective-permute-start.2 = (bf16[4,1056,128]{2,1,0:T(8,128)(2,1)}, bf16[4,1056,128]{2,1,0:T(8,128)(2,1)}, u32[]{:S(2)}, u32[]{:S(2)}) collective-permute-start(bf16[4,1056,128]{2,1,0:T(8,128)(2,1)} %collective-permute-done.x1), channel_id=1, source_target_pairs={{0,8},{1,3},{2,10},{3,5},{4,12},{5,7},{6,14},{7,1},{8,16},{9,11},{... | collective-permute-start | bytes 3244040 | tf_op jit(solution)/shard_map/ppermute | solution.py:297
  50.2 1.6 %copy-start.5 = (bf16[4,1024,256]{2,1,0:T(8,128)(2,1)S(1)}, bf16[4,1024,256]{2,1,0:T(8,128)(2,1)}, u32[]{:S(2)}) copy-start(bf16[4,1024,256]{2,1,0:T(8,128)(2,1)} %own_ref) | copy-start | bytes 6291460
  66.7 0.7 copy-start
  67.4 3.5 %copy-start.1 = (bf16[512,256]{1,0:T(8,128)(2,1)S(1)}, bf16[512,256]{1,0:T(8,128)(2,1)}, u32[]{:S(2)}) copy-start(bf16[512,256]{1,0:T(8,128)(2,1)} %copy-done) | copy-start | bytes 786436
  67.4 0.9 %copy-start.2 = (f32[1,1,2,128,128]{4,3,2,1,0:T(8,128)S(1)}, f32[1,1,2,128,128]{4,3,2,1,0:T(8,128)}, u32[]{:S(2)}) copy-start(f32[1,1,2,128,128]{4,3,2,1,0:T(8,128)} %param.12) | copy-start | bytes 393220

commit v5 on v4

--- a/solution.py
+++ b/solution.py
@@ -289,19 +289,18 @@
         ],
         compiler_params=whole,
     )(table, learn_hidden[0], learn_cotangent[0])
-    line, tiles = lax.optimization_barrier((line, tiles))
-    received = lax.all_to_all(tiles, "dp", 0, 0, tiled=True)
-
-    right = lax.ppermute(line, "expert", shifted(1, 1))
-    line, right = lax.optimization_barrier((line, right))
-    far = lax.ppermute(right, "expert", shifted(1, 1))
-    left = lax.ppermute(line, "expert", shifted(1, -1))
-
-    other_weight = lax.ppermute(rollout_weight, "expert", core_swap())
-    line, rollout_scale = lax.optimization_barrier((line, rollout_scale))
+    tiles, rollout_scale = lax.optimization_barrier((tiles, rollout_scale))
     scales = lax.all_gather(
         rollout_scale, "expert", axis_index_groups=both_cores(), tiled=True
     )
+    line, tiles, scales = lax.optimization_barrier((line, tiles, scales))
+    received = lax.all_to_all(tiles, "dp", 0, 0, tiled=True)
+
+    right = lax.ppermute(line, "expert", shifted(1, 1))
+    left = lax.ppermute(line, "expert", shifted(1, -1))
+    far = lax.ppermute(right, "expert", shifted(1, 1))
+
+    other_weight = lax.ppermute(rollout_weight, "expert", core_swap())
     scales = scales.astype(jnp.float32).reshape(CORES * exp_dev, -1)
 
     def cost(lines):

time: 92.7 us -> 92.6 us (level)
  waiting for transfers between devices: 0.61 us -> 2.85 us
  starting transfers between devices: 34.7 us -> 33.2 us
  blocking collectives: 29.2 us -> 28.2 us
    all_gather x1, blocking collectives: 8.33 us -> 1.78 us  [shards(): lax.all_gather(rollout_scale, 'expert', axis_index_groups=both_cores(), t...]
    all_gather x1, blocking collectives: 2.14 us -> 5.69 us  [shards(): lax.all_gather(own_block, 'expert', axis_index_groups=both_cores(), tiled...]
    all_to_all x1, blocking collectives: 18.7 us -> 20.8 us  [shards(): lax.all_to_all(outgoing, 'expert', 0, 0, axis_index_groups=same_core(), t...]
    all_to_all x1, starting transfers between devices: 13.5 us -> 11.6 us  [shards(): received = lax.all_to_all(tiles, 'dp', 0, 0, tiled=True)]
    ppermute x1, waiting for transfers between devices: 0.01 us -> 1.56 us  [shards(): left = lax.ppermute(line, 'expert', shifted(1, -1))]
    ppermute x1, waiting for transfers between devices: 0.01 us -> 1.28 us  [shards(): far = lax.ppermute(right, 'expert', shifted(1, 1))]
  transfers between devices with their start and end apart: 6 -> 6, of which waited for: 1 -> 2; matrix products, arithmetic and copies ran while one was open for 0% -> 0% of each run, Pallas kernels for 20% -> 20%
where the time goes in v5:
time: 92.6 us; the launch traced here: 91.7 us
  starting transfers between devices  33.2 us (36%)
  blocking collectives  28.2 us (30%)
  Pallas kernels  23.1 us (25%)
  local copies, waits for them, and re-layouts  3.4 us (4%)
  waiting for transfers between devices  2.85 us (3%)
    all_to_all x1, blocking collectives, shards(): lax.all_to_all(outgoing, 'expert', 0, 0, axis_index_groups=same_core(), t...  20.8 us
    all_to_all x1, starting transfers between devices, shards(): received = lax.all_to_all(tiles, 'dp', 0, 0, tiled=True)  11.6 us
    ppermute x1, starting transfers between devices, shards(): other_weight = lax.ppermute(rollout_weight, 'expert', core_swap())  7.48 us
    pallas_call x2, Pallas kernels, add_line(): pl.pallas_call(line_kernel, out_shape=sums_of(1), in_specs=[smem()] * 2 +...  7.48 us
    pallas_call x1, Pallas kernels, shards(): pl.pallas_call(first_kernel, out_shape=(jax.ShapeDtypeStruct((held,) + ro...  7.43 us
    all_gather x1, blocking collectives, shards(): lax.all_gather(own_block, 'expert', axis_index_groups=both_cores(), tiled...  5.69 us
    all_to_all x1, starting transfers between devices, shards(): lax.all_to_all(chunk, 'expert', 0, 0, axis_index_groups=lines(), tiled=True)  4.85 us
    ppermute x1, starting transfers between devices, shards(): right = lax.ppermute(line, 'expert', shifted(1, 1))  3.72 us
  transfers between devices with their start and end apart: 6, of which 2 were waited for; matrix products, arithmetic and copies ran while one was open for 0% of the time, Pallas kernels for 20%

profile of v5, /device:TPU:1, one launch (start us, length us, event | category | flops | bytes accessed | tf_op | source)
XLA Modules:
  0.0 91.7 jit_solution(4505769485825434721)
XLA Ops:
  0.0 2.8 %shard_map.100 = bf16[4,1056,128]{2,1,0:T(8,128)(2,1)} custom-call(s32[128]{0:T(128)} %slot_ref.9, bf16[2,64,1024]{2,1,0:T(8,128)(2,1)} %token_hbm.1, s32[2,8,64]{2,1,0:T(8,128)} %bitcast.17, f32[2,8,64]{2,1,0:T(8,128)} %bitcast.18), custom_call_target="tpu_custom_call" | custom-call | tf_op jit(solution)/shard_map/pallas_call | solution.py:266
  2.9 4.9 %all-to-all-start = ((bf16[4,1056,128]{2,1,0:T(8,128)(2,1)}), bf16[4,1056,128]{2,1,0:T(8,128)(2,1)S(1)}, u32[]{:S(2)}, u32[]{:S(2)}) async-start(bf16[4,1056,128]{2,1,0:T(8,128)(2,1)} %shard_map.100), calls=%async_computation | async-start | bytes 2162688 | tf_op jit(solution)/shard_map/all_to_all | solution.py:278
  7.7 7.5 %collective-permute-start = (bf16[4,1024,256]{2,1,0:T(8,128)(2,1)}, bf16[4,1024,256]{2,1,0:T(8,128)(2,1)}, u32[]{:S(2)}, u32[]{:S(2)}) collective-permute-start(bf16[4,1024,256]{2,1,0:T(8,128)(2,1)} %own_ref), channel_id=1, source_target_pairs={{0,1},{1,0},{2,3},{3,2},{4,5},{5,4},{6,7},{7,6},{8,9},{9,8},{10,11... | collective-permute-start | bytes 6291464 | tf_op jit(solution)/shard_map/ppermute | solution.py:303
  15.2 3.4 %shard_map.101 = bf16[16,2,2,32,128]{4,3,2,1,0:T(8,128)(2,1)} custom-call(s32[16,2,32]{2,1,0:T(2,128)} %bitcast.9, bf16[4,32,1024]{2,1,0:T(8,128)(2,1)} %bitcast.15, bf16[4,32,4096]{2,1,0:T(8,128)(2,1)} %bitcast.14), custom_call_target="tpu_custom_call" | custom-call | tf_op jit(solution)/shard_map/pallas_call | solution.py:280
  18.6 1.8 %all_gather.6 = bf16[8,8,2]{1,2,0:T(2,128)(2,1)S(1)} all-gather(bf16[4,8,2]{1,2,0:T(2,128)(2,1)S(1)} %copy-done.6), channel_id=1, replica_groups={{0,1},{2,3},{4,5},{6,7},{8,9},{10,11},{12,13},{14,15},{16,17},{18,19},{..., dimensions={0}, use_global_device_ids=true | all-gather | bytes 384 | tf_op jit(solution)/shard_map/all_gather | solution.py:293
  20.4 3.7 %collective-permute-start.1 = (bf16[4,1056,128]{2,1,0:T(8,128)(2,1)S(1)}, bf16[4,1056,128]{2,1,0:T(8,128)(2,1)}, u32[]{:S(2)}, u32[]{:S(2)}) collective-permute-start(bf16[4,1056,128]{2,1,0:T(8,128)(2,1)S(1)} %all-to-all-done.x0), channel_id=1, source_target_pairs={{0,8},{1,3},{2,10},{3,5},{4,12},{5,7},{6,14},{7,1},{8,16},{9,11},{... | collective-permute-start | bytes 3244040 | tf_op jit(solution)/shard_map/ppermute | solution.py:299
  24.1 11.6 %all-to-all-start.1 = ((bf16[16,2,2,32,128]{4,3,2,1,0:T(8,128)(2,1)}), bf16[16,2,2,32,128]{4,3,2,1,0:T(8,128)(2,1)S(1)}, u32[]{:S(2)}, u32[]{:S(2)}) async-start(bf16[16,2,2,32,128]{4,3,2,1,0:T(8,128)(2,1)} %shard_map.101), calls=%async_computation.1 | async-start | bytes 1048576 | tf_op jit(solution)/shard_map/all_to_all | solution.py:297
  35.8 3.6 %collective-permute-start.3 = (bf16[4,1056,128]{2,1,0:T(8,128)(2,1)S(1)}, bf16[4,1056,128]{2,1,0:T(8,128)(2,1)}, u32[]{:S(2)}, u32[]{:S(2)}) collective-permute-start(bf16[4,1056,128]{2,1,0:T(8,128)(2,1)S(1)} %all-to-all-done.x0), channel_id=1, source_target_pairs={{0,24},{1,7},{2,26},{3,1},{4,28},{5,3},{6,30},{7,5},{8,0},{9,15},{... | collective-permute-start | bytes 3244040 | tf_op jit(solution)/shard_map/ppermute | solution.py:300
  39.4 1.9 %collective-permute-start.2 = (bf16[4,1056,128]{2,1,0:T(8,128)(2,1)}, bf16[4,1056,128]{2,1,0:T(8,128)(2,1)}, u32[]{:S(2)}, u32[]{:S(2)}) collective-permute-start(bf16[4,1056,128]{2,1,0:T(8,128)(2,1)} %collective-permute-done.1.x1), channel_id=1, source_target_pairs={{0,8},{1,3},{2,10},{3,5},{4,12},{5,7},{6,14},{7,1},{8,16},{9,11},{... | collective-permute-start | bytes 3244040 | tf_op jit(solution)/shard_map/ppermute | solution.py:301
  41.3 0.1 copy.13
  41.4 0.1 copy.14.scale_ref
  41.5 1.6 %copy-done.5 = bf16[4,1024,256]{2,1,0:T(8,128)(2,1)S(1)} copy-done((bf16[4,1024,256]{2,1,0:T(8,128)(2,1)S(1)}, bf16[4,1024,256]{2,1,0:T(8,128)(2,1)}, u32[]{:S(2)}) %copy-start.5) | copy-done | bytes 2097176
  43.1 7.4 %shard_map.102 = (bf16[8,1024,256]{2,1,0:T(8,128)(2,1)S(1)}, bf16[1024,256]{1,0:T(8,128)(2,1)S(1)}, bf16[1024,512]{1,0:T(8,128)(2,1)S(1)}) custom-call(s32[16,2,32]{2,1,0:T(2,128)S(1)} %bitcast.10, s32[128]{0:T(128)S(1)} %copy-done.4, f32[8,16]{1,0:T(8,128)S(1)} %copy.14.scale_ref, bf16[4,1024,256]{2,1,0:T(8,128)(2,1)S(1)} %copy-done.5, ...), custom_call_target="tpu_custom_call" | custom-call | flops 4294967296 | bytes 12582912 | tf_op jit(solution)/shard_map/pallas_call | solution.py:320
  50.5 1.6 %collective-permute-done.3.x_ref = bf16[4,1056,128]{2,1,0:T(8,128)(2,1)} collective-permute-done((bf16[4,1056,128]{2,1,0:T(8,128)(2,1)S(1)}, bf16[4,1056,128]{2,1,0:T(8,128)(2,1)}, u32[]{:S(2)}, u32[]{:S(2)}) %collective-permute-start.3) | collective-permute-done | bytes 1081376 | tf_op jit(solution)/shard_map/ppermute | solution.py:300
  52.1 3.7 %shard_map.103 = (bf16[512,256]{1,0:T(8,128)(2,1)S(1)}, bf16[512,512]{1,0:T(8,128)(2,1)S(1)}) custom-call(s32[16,2,32]{2,1,0:T(2,128)S(1)} %bitcast.11, s32[128]{0:T(128)S(1)} %copy-done.4, bf16[8,1024,256]{2,1,0:T(8,128)(2,1)S(1)} %get-tuple-element.36.weight_ref, bf16[4,1056,128]{2,1,0:T(8,128)(2,1)} %collective-permute-done.3.x_ref), custom_call_target="tpu_custom_call" | custom-call | flops 2147483648 | bytes 6291456 | tf_op jit(solution)/shard_map/pallas_call | solution.py:332
  55.8 1.3 %collective-permute-done.2.x_ref = bf16[4,1056,128]{2,1,0:T(8,128)(2,1)} collective-permute-done((bf16[4,1056,128]{2,1,0:T(8,128)(2,1)}, bf16[4,1056,128]{2,1,0:T(8,128)(2,1)}, u32[]{:S(2)}, u32[]{:S(2)}) %collective-permute-start.2) | collective-permute-done | bytes 1081376 | tf_op jit(solution)/shard_map/ppermute | solution.py:301
  57.1 3.7 %shard_map.104 = (bf16[512,256]{1,0:T(8,128)(2,1)S(1)}, bf16[512,512]{1,0:T(8,128)(2,1)S(1)}) custom-call(s32[16,2,32]{2,1,0:T(2,128)S(1)} %bitcast.12, s32[128]{0:T(128)S(1)} %copy-done.4, bf16[8,1024,256]{2,1,0:T(8,128)(2,1)S(1)} %get-tuple-element.36.weight_ref, bf16[4,1056,128]{2,1,0:T(8,128)(2,1)} %collective-permute-done.2.x_ref), custom_call_target="tpu_custom_call" | custom-call | flops 2147483648 | bytes 6291456 | tf_op jit(solution)/shard_map/pallas_call | solution.py:332
  60.8 0.7 copy-done
  61.5 0.9 %copy-done.2 = f32[1,1,2,128,128]{4,3,2,1,0:T(8,128)S(1)} copy-done((f32[1,1,2,128,128]{4,3,2,1,0:T(8,128)S(1)}, f32[1,1,2,128,128]{4,3,2,1,0:T(8,128)}, u32[]{:S(2)}) %copy-start.2) | copy-done | bytes 131096
  62.5 0.4 shard_map.105
  62.8 5.7 %all_gather.7.block_ref = bf16[4,144,128]{2,1,0:T(8,128)(2,1)S(1)} all-gather(bf16[2,144,128]{2,1,0:T(8,128)(2,1)S(1)} %shard_map.105), channel_id=1, replica_groups={{0,1},{2,3},{4,5},{6,7},{8,9},{10,11},{12,13},{14,15},{16,17},{18,19},{..., dimensions={0}, use_global_device_ids=true | all-gather | bytes 221184 | tf_op jit(solution)/shard_map/all_gather | solution.py:355
  68.5 1.6 %shard_map.106 = bf16[16,128,256]{2,1,0:T(8,128)(2,1)S(1)} custom-call(s32[16,2,32]{2,1,0:T(2,128)S(1)} %bitcast.13, s32[128]{0:T(128)S(1)} %copy-done.4, bf16[4,144,128]{2,1,0:T(8,128)(2,1)S(1)} %all_gather.7.block_ref, bf16[1024,256]{1,0:T(8,128)(2,1)S(1)} %get-tuple-element.43.s0, bf16[512,256]{1,0:T(8,128)(2,1)S(1)} %get-tuple-element.44.s1, ...), custom_call_target="tpu_custom_call" | custom-call | tf_op jit(solution)/shard_map/pallas_call | solution.py:357
  70.1 20.8 %all_to_all.15 = bf16[16,128,256]{2,1,0:T(8,128)(2,1)S(1)} all-to-all(bf16[16,128,256]{2,1,0:T(8,128)(2,1)S(1)} %shard_map.106), channel_id=1, replica_groups={{0,2,4,6,8,10,12,14,16,18,20,22,24,26,28,30},{1,3,5,7,9,11,13,15,17,19,..., dimensions={0} | all-to-all | bytes 2097152 | tf_op jit(solution)/shard_map/all_to_all | solution.py:369
  90.9 0.8 reduce_sum.12
  (15 shorter events, 0.0 us)
Async XLA Ops:
  2.9 17.5 %all-to-all-start = ((bf16[4,1056,128]{2,1,0:T(8,128)(2,1)}), bf16[4,1056,128]{2,1,0:T(8,128)(2,1)S(1)}, u32[]{:S(2)}, u32[]{:S(2)}) async-start(bf16[4,1056,128]{2,1,0:T(8,128)(2,1)} %shard_map.100), calls=%async_computation | async-start | bytes 2162688 | tf_op jit(solution)/shard_map/all_to_all | solution.py:278
  7.7 10.9 %copy-start.6 = (bf16[4,8,2]{1,2,0:T(2,128)(2,1)S(1)}, bf16[4,8,2]{1,2,0:T(2,128)(2,1)}, u32[]{:S(2)}) copy-start(bf16[4,8,2]{1,2,0:T(2,128)(2,1)} %param.16) | copy-start | bytes 388
  7.7 33.7 %collective-permute-start = (bf16[4,1024,256]{2,1,0:T(8,128)(2,1)}, bf16[4,1024,256]{2,1,0:T(8,128)(2,1)}, u32[]{:S(2)}, u32[]{:S(2)}) collective-permute-start(bf16[4,1024,256]{2,1,0:T(8,128)(2,1)} %own_ref), channel_id=1, source_target_pairs={{0,1},{1,0},{2,3},{3,2},{4,5},{5,4},{6,7},{7,6},{8,9},{9,8},{10,11... | collective-permute-start | bytes 6291464 | tf_op jit(solution)/shard_map/ppermute | solution.py:303
  15.2 26.3 %copy-start.3 = (s32[32,16,2]{0,2,1:T(2,128)S(1)}, s32[32,16,2]{0,2,1:T(2,128)}, u32[]{:S(2)}) copy-start(s32[32,16,2]{0,2,1:T(2,128)} %param.13) | copy-start | bytes 12292
  15.2 26.2 %copy-start.4 = (s32[128]{0:T(128)S(1)}, s32[128]{0:T(128)}, u32[]{:S(2)}) copy-start(s32[128]{0:T(128)} %slot_ref.9) | copy-start | bytes 1540
  20.4 19.0 %collective-permute-start.1 = (bf16[4,1056,128]{2,1,0:T(8,128)(2,1)S(1)}, bf16[4,1056,128]{2,1,0:T(8,128)(2,1)}, u32[]{:S(2)}, u32[]{:S(2)}) collective-permute-start(bf16[4,1056,128]{2,1,0:T(8,128)(2,1)S(1)} %all-to-all-done.x0), channel_id=1, source_target_pairs={{0,8},{1,3},{2,10},{3,5},{4,12},{5,7},{6,14},{7,1},{8,16},{9,11},{... | collective-permute-start | bytes 3244040 | tf_op jit(solution)/shard_map/ppermute | solution.py:299
  24.1 37.4 %all-to-all-start.1 = ((bf16[16,2,2,32,128]{4,3,2,1,0:T(8,128)(2,1)}), bf16[16,2,2,32,128]{4,3,2,1,0:T(8,128)(2,1)S(1)}, u32[]{:S(2)}, u32[]{:S(2)}) async-start(bf16[16,2,2,32,128]{4,3,2,1,0:T(8,128)(2,1)} %shard_map.101), calls=%async_computation.1 | async-start | bytes 1048576 | tf_op jit(solution)/shard_map/all_to_all | solution.py:297
  35.8 16.3 %collective-permute-start.3 = (bf16[4,1056,128]{2,1,0:T(8,128)(2,1)S(1)}, bf16[4,1056,128]{2,1,0:T(8,128)(2,1)}, u32[]{:S(2)}, u32[]{:S(2)}) collective-permute-start(bf16[4,1056,128]{2,1,0:T(8,128)(2,1)S(1)} %all-to-all-done.x0), channel_id=1, source_target_pairs={{0,24},{1,7},{2,26},{3,1},{4,28},{5,3},{6,30},{7,5},{8,0},{9,15},{... | collective-permute-start | bytes 3244040 | tf_op jit(solution)/shard_map/ppermute | solution.py:300
  39.4 17.7 %collective-permute-start.2 = (bf16[4,1056,128]{2,1,0:T(8,128)(2,1)}, bf16[4,1056,128]{2,1,0:T(8,128)(2,1)}, u32[]{:S(2)}, u32[]{:S(2)}) collective-permute-start(bf16[4,1056,128]{2,1,0:T(8,128)(2,1)} %collective-permute-done.1.x1), channel_id=1, source_target_pairs={{0,8},{1,3},{2,10},{3,5},{4,12},{5,7},{6,14},{7,1},{8,16},{9,11},{... | collective-permute-start | bytes 3244040 | tf_op jit(solution)/shard_map/ppermute | solution.py:301
  41.5 1.6 %copy-start.5 = (bf16[4,1024,256]{2,1,0:T(8,128)(2,1)S(1)}, bf16[4,1024,256]{2,1,0:T(8,128)(2,1)}, u32[]{:S(2)}) copy-start(bf16[4,1024,256]{2,1,0:T(8,128)(2,1)} %own_ref) | copy-start | bytes 6291460
  60.8 0.7 copy-start
  61.5 7.0 %copy-start.1 = (bf16[512,256]{1,0:T(8,128)(2,1)S(1)}, bf16[512,256]{1,0:T(8,128)(2,1)}, u32[]{:S(2)}) copy-start(bf16[512,256]{1,0:T(8,128)(2,1)} %copy-done) | copy-start | bytes 786436
  61.5 0.9 %copy-start.2 = (f32[1,1,2,128,128]{4,3,2,1,0:T(8,128)S(1)}, f32[1,1,2,128,128]{4,3,2,1,0:T(8,128)}, u32[]{:S(2)}) copy-start(f32[1,1,2,128,128]{4,3,2,1,0:T(8,128)} %param.12) | copy-start | bytes 393220
